TPU v7x, 256 devices: a whole 4x4x8 slice. The times are simulated.
256 devices in a mesh: dp: 8 (over z), expert: 32 (over x, y, core).
Axes of the slice: x: 4, y: 4, z: 8, core: 2. Of those that a mesh axis runs over, the one named last changes fastest.
Arguments:
- tokens: bfloat16 [65536, 2048], P(('dp', 'expert')), may hold values from -6 to 6
- chosen_expert_index: int32 [65536, 8], P(('dp', 'expert')), may hold values from 0 to 127, as said below
- routing_gate_weight: float32 [65536, 8], P(('dp', 'expert')), may hold values from 0.1 to 1
- w_gate: bfloat16 [32, 2048, 768], P('expert'), may hold values from -0.125 to 0.125
- w_up: bfloat16 [32, 2048, 768], P('expert'), may hold values from -0.125 to 0.125
- w_down: bfloat16 [32, 768, 2048], P('expert'), may hold values from -0.21875 to 0.21875
- capacity: int32 [8, 32], P('dp', 'expert'), may hold values from 128 to 768, as said below
Outputs:
- mixed: bfloat16 [65536, 2048], P(('dp', 'expert'))
Inputs may be any that keep to these rules, and one draw needn't show every extreme that they name: `chosen_expert_index`: slot k of a token names an expert among 16 k to 16 k + 15, so a token's experts differ. Among the rows of one device no expert is named by more than 32 rows, and some expert in flight is named by exactly 32 rows of each device. Some group and expert have capacity 768 in every draw.
All inputs are finite; a program needn't handle non-finite values.
Results may differ from a plain program's by a relative error of at most 0.0058.
Values may be sent and summed in bfloat16 or wider, within the bound.
A program may use at most 64 MiB of HBM per device.

v0:
```python
import jax
import jax.numpy as jnp
from jax import lax
from jax.sharding import PartitionSpec as P

BLOCK = 128


def from_partner(value, axis, bit):
    mask = 2**bit
    pairs = [(source, source ^ mask) for source in range(lax.axis_size(axis))]
    return lax.ppermute(value, axis, pairs)


def expert_ffn(rows, w_gate, w_up, w_down):
    gated = jnp.dot(rows, w_gate[0], preferred_element_type=jnp.float32)
    upward = jnp.dot(rows, w_up[0], preferred_element_type=jnp.float32)
    hidden = (jax.nn.silu(gated) * upward).astype(jnp.bfloat16)
    return jnp.dot(hidden, w_down[0], preferred_element_type=jnp.float32)


def on_device(tokens, chosen_expert_index, routing_gate_weight, w_gate, w_up, w_down, capacity):
    resident_experts = lax.axis_size("expert")
    tok_rows = tokens.shape[0]
    width = tokens.shape[1]
    capacity_positions = tok_rows // 8
    block = BLOCK
    partner_bit = lax.axis_size("dp").bit_length() - 2
    targets = jnp.arange(resident_experts, dtype=jnp.int32)
    matches = chosen_expert_index[:, :, None] == targets[None, None, :]
    chosen = jnp.any(matches, axis=1)
    chosen_int = chosen.astype(jnp.int32)
    position = jnp.cumsum(chosen_int, axis=0) - 1
    counts = jnp.sum(chosen_int, axis=0)
    slot_ids = jnp.arange(capacity_positions, dtype=jnp.int32)
    placer = (position.T[:, None, :] == slot_ids[None, :, None]) & chosen.T[:, None, :]
    send_rows = jnp.einsum(
        "jpt,td->jpd", placer.astype(jnp.bfloat16), tokens, preferred_element_type=jnp.float32
    ).astype(jnp.bfloat16)
    arrived, arrived_counts = (
        lax.all_to_all(send_rows, "expert", split_axis=0, concat_axis=0, tiled=True),
        lax.all_to_all(counts[:, None], "expert", split_axis=0, concat_axis=0, tiled=True),
    )
    arrived_counts = arrived_counts[:, 0]
    offsets = jnp.cumsum(arrived_counts) - arrived_counts
    load = jnp.sum(arrived_counts)
    limit = capacity[0, 0]
    spare = jnp.maximum(limit - load, 0)
    ranks = (offsets[:, None] + slot_ids[None, :]).reshape(-1)
    valid = (slot_ids[None, :] < arrived_counts[:, None]).reshape(-1)
    flat_rows = arrived.reshape(resident_experts * capacity_positions, width)
    home_keep = valid & (ranks < limit)
    over_index = ranks - limit
    over_sel = valid & (over_index >= 0) & (over_index < block)
    block_ids = jnp.arange(block, dtype=jnp.int32)
    picker = ((over_index[None, :] == block_ids[:, None]) & over_sel[None, :]).astype(jnp.bfloat16)
    overflow = jnp.dot(picker, flat_rows, preferred_element_type=jnp.float32).astype(jnp.bfloat16)
    extra_rows = from_partner(overflow, "dp", partner_bit)
    extra_keep = block_ids < spare
    all_rows = jnp.concatenate([flat_rows, extra_rows], axis=0)
    all_keep = jnp.concatenate([home_keep, extra_keep], axis=0)
    computed = expert_ffn(all_rows, w_gate, w_up, w_down)
    outputs = jnp.where(all_keep[:, None], computed, 0.0).astype(jnp.bfloat16)
    home_out = outputs[: resident_experts * capacity_positions]
    extra_out = outputs[resident_experts * capacity_positions :]
    returned = from_partner(extra_out, "dp", partner_bit)
    placed = jnp.einsum("of,od->fd", picker, returned, preferred_element_type=jnp.float32).astype(
        jnp.bfloat16
    )
    answers = jnp.where(over_sel[:, None], placed, home_out).reshape(
        resident_experts, capacity_positions, width
    )
    back = lax.all_to_all(answers, "expert", split_axis=0, concat_axis=0, tiled=True)
    pending_transfer = chosen_expert_index < resident_experts
    routing_position = jnp.sum(jnp.where(matches, position[:, None, :], 0), axis=2)
    flattened_index = jnp.where(
        pending_transfer, chosen_expert_index * capacity_positions + routing_position, 0
    )
    gathered = jnp.take(
        back.reshape(resident_experts * capacity_positions, width), flattened_index, axis=0
    )
    combine_scale = jnp.where(pending_transfer, routing_gate_weight, 0.0)
    mixed = jnp.sum(combine_scale[:, :, None] * gathered.astype(jnp.float32), axis=1)
    return mixed.astype(jnp.bfloat16)


def solution(mesh):
    return jax.shard_map(
        on_device,
        mesh=mesh,
        in_specs=(
            P(("dp", "expert"), None),
            P(("dp", "expert"), None),
            P(("dp", "expert"), None),
            P("expert", None, None),
            P("expert", None, None),
            P("expert", None, None),
            P("dp", "expert"),
        ),
        out_specs=P(("dp", "expert"), None),
        check_vma=False,
    )
```

profile of v0, /device:TPU:1, one launch (start us, length us, event | category | flops | bytes accessed | tf_op | source)
XLA Modules:
  0.0 241.0 jit_solution(15631488022258071852)
XLA Ops:
  0.0 0.9 fusion.17
  1.0 0.7 copy.43
  1.7 8.6 %all-to-all-start = ((s32[32,1,1]{2,1,0:T(1,128)}), s32[32,1,1]{2,1,0:T(1,128)S(1)}, u32[]{:S(2)}, u32[]{:S(2)}) async-start(s32[32,1,1]{2,1,0:T(1,128)} %copy.43), calls=%async_computation | async-start | bytes 32768 | tf_op jit(solution)/shard_map/all_to_all | solution.py:42
  10.3 0.6 reduce-window.18
  10.9 0.2 slice_reduce_fusion
  11.2 4.5 %convolution_convert_fusion = bf16[32,32,2048]{2,1,0:T(8,128)(2,1)} fusion(bf16[256,2048]{1,0:T(8,128)(2,1)} %param.7, s32[32,256]{1,0:T(8,128)S(1)} %get-tuple-element.10, pred[32,256]{1,0:T(8,128)(4,1)S(1)} %bitcast.49), kind=kOutput, calls=%fused_computation.6 | convolution fusion | flops 1076363264 | bytes 5283840 | tf_op jit(solution)/shard_map/jpt,td->jpd/dot_general | solution.py:37
  15.7 1.5 all-to-all-done
  17.2 6.0 %all-to-all-start.1 = ((bf16[32,32,2048]{2,1,0:T(8,128)(2,1)}), bf16[32,32,2048]{2,1,0:T(8,128)(2,1)}, u32[]{:S(2)}, u32[]{:S(2)}) async-start(bf16[32,32,2048]{2,1,0:T(8,128)(2,1)} %convolution_convert_fusion), calls=%async_computation.1 | async-start | bytes 8388608 | tf_op jit(solution)/shard_map/all_to_all | solution.py:41
  23.9 1.2 fusion.25
  25.7 49.7 %all-to-all-done.1 = bf16[32,32,2048]{2,1,0:T(8,128)(2,1)} async-done(((bf16[32,32,2048]{2,1,0:T(8,128)(2,1)}), bf16[32,32,2048]{2,1,0:T(8,128)(2,1)}, u32[]{:S(2)}, u32[]{:S(2)}) %all-to-all-start.1) | async-done | bytes 4194336 | tf_op jit(solution)/shard_map/all_to_all | solution.py:41
  75.3 3.7 %convolution_convert_fusion.1 = bf16[128,2048]{1,0:T(8,128)(2,1)} fusion(bf16[1024,2048]{1,0:T(8,128)(2,1)} %bitcast.6, s32[1024]{0:T(1024)S(1)} %sub.44, pred[1024]{0:T(1024)(128)(4,1)S(1)} %get-tuple-element.12), kind=kOutput, calls=%fused_computation.13 | convolution fusion | flops 537395200 | bytes 4723712 | tf_op jit(solution)/shard_map/dot_general | solution.py:57
  79.0 6.9 %collective-permute-start = (bf16[128,2048]{1,0:T(8,128)(2,1)}, bf16[128,2048]{1,0:T(8,128)(2,1)}, u32[]{:S(2)}, u32[]{:S(2)}) collective-permute-start(bf16[128,2048]{1,0:T(8,128)(2,1)} %convolution_convert_fusion.1), channel_id=1, source_target_pairs={{0,128},{32,160},{64,192},{96,224},{128,0},{160,32},{192,64},{224,... | collective-permute-start | bytes 1572872 | tf_op jit(solution)/shard_map/ppermute | solution.py:12
  86.6 13.2 %collective-permute-done = bf16[128,2048]{1,0:T(8,128)(2,1)} collective-permute-done((bf16[128,2048]{1,0:T(8,128)(2,1)}, bf16[128,2048]{1,0:T(8,128)(2,1)}, u32[]{:S(2)}, u32[]{:S(2)}) %collective-permute-start) | collective-permute-done | bytes 524320 | tf_op jit(solution)/shard_map/ppermute | solution.py:12
  99.8 7.0 %fusion.5 = f32[1152,768]{1,0:T(8,128)S(1)} fusion(bf16[1,2048,768]{2,1,0:T(8,128)(2,1)} %param.10, bf16[128,2048]{1,0:T(8,128)(2,1)} %collective-permute-done, bf16[1024,2048]{1,0:T(8,128)(2,1)} %bitcast.6), kind=kOutput, calls=%fused_computation.11 | convolution fusion | flops 3633315840 | bytes 11403264 | tf_op jit(solution)/shard_map/dot_general | solution.py:16
  106.8 6.7 %multiply_convert_fusion = bf16[1152,768]{1,0:T(8,128)(2,1)S(1)} fusion(f32[1152,768]{1,0:T(8,128)S(1)} %fusion.5, bf16[1,2048,768]{2,1,0:T(8,128)(2,1)S(1)} %copy-done.3, bf16[128,2048]{1,0:T(8,128)(2,1)} %collective-permute-done, bf16[1024,2048]{1,0:T(8,128)(2,1)} %bitcast.6), kind=kOutput, calls=%fused_computation.7 | convolution fusion | flops 3638624256 | bytes 13172736 | tf_op jit(solution)/shard_map/dot_general | solution.py:17
  113.5 4.1 %select_convert_fusion = bf16[1152,2048]{1,0:T(8,128)(2,1)S(1)} fusion(bf16[1152,768]{1,0:T(8,128)(2,1)S(1)} %multiply_convert_fusion, pred[1152]{0:T(1024)(128)(4,1)S(1)} %pad_add_fusion, bf16[1,768,2048]{2,1,0:T(8,128)(2,1)S(1)} %copy-done), kind=kOutput, calls=%fused_computation.2 | convolution fusion | flops 3628597248 | bytes 9634944 | tf_op jit(solution)/shard_map/dot_general | solution.py:19
  117.6 5.4 %collective-permute-start.1 = (bf16[128,2048]{1,0:T(8,128)(2,1)S(1)}, bf16[128,2048]{1,0:T(8,128)(2,1)S(1)}, u32[]{:S(2)}, u32[]{:S(2)}) collective-permute-start(bf16[128,2048]{1,0:T(8,128)(2,1)S(1)} %slice.19), channel_id=1, source_target_pairs={{0,128},{32,160},{64,192},{96,224},{128,0},{160,32},{192,64},{224,... | collective-permute-start | bytes 1572872 | tf_op jit(solution)/shard_map/ppermute | solution.py:12
  123.0 6.8 %collective-permute-done.1 = bf16[128,2048]{1,0:T(8,128)(2,1)S(1)} collective-permute-done((bf16[128,2048]{1,0:T(8,128)(2,1)S(1)}, bf16[128,2048]{1,0:T(8,128)(2,1)S(1)}, u32[]{:S(2)}, u32[]{:S(2)}) %collective-permute-start.1) | collective-permute-done | bytes 524320 | tf_op jit(solution)/shard_map/ppermute | solution.py:12
  129.8 2.9 %slice_select_fusion = bf16[1024,2048]{1,0:T(8,128)(2,1)} fusion(bf16[1152,2048]{1,0:T(8,128)(2,1)S(1)} %select_convert_fusion, pred[1024]{0:T(1024)(128)(4,1)S(1)} %get-tuple-element.12, bf16[128,2048]{1,0:T(8,128)(2,1)S(1)} %collective-permute-done.1, s32[1024]{0:T(1024)S(1)} %sub.44), kind=kOutput, calls=%fused_computation.5 | convolution fusion | flops 541327360 | bytes 8919040 | tf_op jit(solution)/shard_map/of,od->fd/dot_general | solution.py:67
  132.7 26.6 %all-to-all-start.2 = ((bf16[32,32,2048]{2,1,0:T(8,128)(2,1)}), bf16[32,32,2048]{2,1,0:T(8,128)(2,1)}, u32[]{:S(2)}, u32[]{:S(2)}) async-start(bf16[32,32,2048]{2,1,0:T(8,128)(2,1)} %bitcast.47), calls=%async_computation.2 | async-start | bytes 8388608 | tf_op jit(solution)/shard_map/all_to_all | solution.py:73
  159.7 0.2 copy.42
  160.0 51.6 %all-to-all-done.2 = bf16[32,32,2048]{2,1,0:T(8,128)(2,1)} async-done(((bf16[32,32,2048]{2,1,0:T(8,128)(2,1)}), bf16[32,32,2048]{2,1,0:T(8,128)(2,1)}, u32[]{:S(2)}, u32[]{:S(2)}) %all-to-all-start.2) | async-done | bytes 4194336 | tf_op jit(solution)/shard_map/all_to_all | solution.py:73
  211.6 19.1 %gather_fusion = bf16[2048,2048]{1,0:T(8,128)(2,1)} fusion(bf16[1024,2048]{1,0:T(8,128)(2,1)} %bitcast.11, s32[2048]{0:T(1024)S(1)} %broadcast_clamp_fusion), kind=kCustom, calls=%fused_computation | custom fusion | bytes 16785408 | tf_op jit(solution)/shard_map/jit(_take)/gather | solution.py:79
  230.6 10.3 %multiply_reduce_fusion = bf16[256,2048]{1,0:T(8,128)(2,1)} fusion(bf16[2048,2048]{1,0:T(8,128)(2,1)} %gather_fusion, f32[256,8]{1,0:T(8,128)S(1)} %copy.39, pred[256,8]{1,0:T(8,128)(4,1)S(1)} %copy.42), kind=kLoop, calls=%fused_computation.1 | loop fusion | flops 16252928 | bytes 9447424 | tf_op jit(solution)/shard_map/reduce_sum | solution.py:83
  (33 shorter events, 1.4 us)
Async XLA Ops:
  0.0 113.5 %copy-start = (bf16[1,768,2048]{2,1,0:T(8,128)(2,1)S(1)}, bf16[1,768,2048]{2,1,0:T(8,128)(2,1)}, u32[]{:S(2)}) copy-start(bf16[1,768,2048]{2,1,0:T(8,128)(2,1)} %param.12) | copy-start | bytes 9437188
  1.7 15.5 %all-to-all-start = ((s32[32,1,1]{2,1,0:T(1,128)}), s32[32,1,1]{2,1,0:T(1,128)S(1)}, u32[]{:S(2)}, u32[]{:S(2)}) async-start(s32[32,1,1]{2,1,0:T(1,128)} %copy.43), calls=%async_computation | async-start | bytes 32768 | tf_op jit(solution)/shard_map/all_to_all | solution.py:42
  17.2 58.2 %all-to-all-start.1 = ((bf16[32,32,2048]{2,1,0:T(8,128)(2,1)}), bf16[32,32,2048]{2,1,0:T(8,128)(2,1)}, u32[]{:S(2)}, u32[]{:S(2)}) async-start(bf16[32,32,2048]{2,1,0:T(8,128)(2,1)} %convolution_convert_fusion), calls=%async_computation.1 | async-start | bytes 8388608 | tf_op jit(solution)/shard_map/all_to_all | solution.py:41
  79.0 20.7 %collective-permute-start = (bf16[128,2048]{1,0:T(8,128)(2,1)}, bf16[128,2048]{1,0:T(8,128)(2,1)}, u32[]{:S(2)}, u32[]{:S(2)}) collective-permute-start(bf16[128,2048]{1,0:T(8,128)(2,1)} %convolution_convert_fusion.1), channel_id=1, source_target_pairs={{0,128},{32,160},{64,192},{96,224},{128,0},{160,32},{192,64},{224,... | collective-permute-start | bytes 1572872 | tf_op jit(solution)/shard_map/ppermute | solution.py:12
  86.6 20.2 %copy-start.3 = (bf16[1,2048,768]{2,1,0:T(8,128)(2,1)S(1)}, bf16[1,2048,768]{2,1,0:T(8,128)(2,1)}, u32[]{:S(2)}) copy-start(bf16[1,2048,768]{2,1,0:T(8,128)(2,1)} %param.11) | copy-start | bytes 9437188
  117.6 12.2 %collective-permute-start.1 = (bf16[128,2048]{1,0:T(8,128)(2,1)S(1)}, bf16[128,2048]{1,0:T(8,128)(2,1)S(1)}, u32[]{:S(2)}, u32[]{:S(2)}) collective-permute-start(bf16[128,2048]{1,0:T(8,128)(2,1)S(1)} %slice.19), channel_id=1, source_target_pairs={{0,128},{32,160},{64,192},{96,224},{128,0},{160,32},{192,64},{224,... | collective-permute-start | bytes 1572872 | tf_op jit(solution)/shard_map/ppermute | solution.py:12
  132.7 26.7 %copy-start.1 = (s32[256,8]{0,1:T(8,128)S(1)}, s32[256,8]{0,1:T(8,128)}, u32[]{:S(2)}) copy-start(s32[256,8]{0,1:T(8,128)} %param.8) | copy-start | bytes 24580
  132.7 27.1 %copy-start.2 = (f32[256,8]{0,1:T(8,128)S(1)}, f32[256,8]{0,1:T(8,128)}, u32[]{:S(2)}) copy-start(f32[256,8]{0,1:T(8,128)} %param.9) | copy-start | bytes 24580
  132.7 78.9 %all-to-all-start.2 = ((bf16[32,32,2048]{2,1,0:T(8,128)(2,1)}), bf16[32,32,2048]{2,1,0:T(8,128)(2,1)}, u32[]{:S(2)}, u32[]{:S(2)}) async-start(bf16[32,32,2048]{2,1,0:T(8,128)(2,1)} %bitcast.47), calls=%async_computation.2 | async-start | bytes 8388608 | tf_op jit(solution)/shard_map/all_to_all | solution.py:73
where the time goes:
time: 246 us; the launch traced here: 241 us
  waiting for transfers between devices  123 us (50%)
  starting transfers between devices  53.5 us (22%)
  matrix products  28.8 us (12%)
  local copies, waits for them, and re-layouts  20.8 us (8%)
  other arithmetic  13.8 us (6%)
    all_to_all x1, waiting for transfers between devices, on_device(): lax.all_to_all(answers, 'expert', split_axis=0, concat_axis=0, tiled=True)  51.6 us
    all_to_all x1, waiting for transfers between devices, on_device(): lax.all_to_all(send_rows, 'expert', split_axis=0, concat_axis=0, tiled=True)  49.7 us
    all_to_all x1, starting transfers between devices, on_device(): lax.all_to_all(answers, 'expert', split_axis=0, concat_axis=0, tiled=True)  26.6 us
    ppermute x2, waiting for transfers between devices, from_partner(): return lax.ppermute(value, axis, pairs)  20 us
    gather x1, local copies, waits for them, and re-layouts, on_device(): jnp.take(back.reshape(resident_experts * capacity_positions, width), flat...  19.1 us
    ppermute x2, starting transfers between devices, from_partner(): return lax.ppermute(value, axis, pairs)  12.3 us
    reduce_sum x1, other arithmetic, on_device(): jnp.sum(combine_scale[:, :, None] * gathered.astype(jnp.float32), axis=1)  10.3 us
    all_to_all x1, starting transfers between devices, on_device(): lax.all_to_all(counts[:, None], 'expert', split_axis=0, concat_axis=0, ti...  8.59 us
  transfers between devices with their start and end apart: 5, of which 5 were waited for; matrix products, arithmetic and copies ran while one was open for 3% of the time, Pallas kernels for 0%

commit v1 on v0

v1 whole, which is shorter than its diff:
```python
import jax
import jax.numpy as jnp
from jax import lax
from jax.sharding import PartitionSpec as P

BLOCK = 128
SLOT = 32


def on_device(tokens, chosen_expert_index, routing_gate_weight, w_gate, w_up, w_down, capacity):
    experts = lax.axis_size("expert")
    groups = lax.axis_size("dp")
    width = tokens.shape[1]
    slots = experts // 16
    targets = jnp.arange(experts, dtype=jnp.int32)
    matches = chosen_expert_index[:, :slots, None] == targets[None, None, :]
    chosen = jnp.any(matches, axis=1)
    weight = jnp.sum(jnp.where(matches, routing_gate_weight[:, :slots, None], 0.0), axis=1)
    chosen_int = chosen.astype(jnp.int32)
    position = jnp.cumsum(chosen_int, axis=0) - 1
    counts = jnp.sum(chosen_int, axis=0)
    slot_ids = jnp.arange(SLOT, dtype=jnp.int32)
    placer = (position.T[:, None, :] == slot_ids[None, :, None]) & chosen.T[:, None, :]
    send_rows = jnp.einsum(
        "jpt,td->jpd", placer.astype(jnp.bfloat16), tokens, preferred_element_type=jnp.float32
    ).astype(jnp.bfloat16)
    arrived = lax.all_to_all(send_rows, "expert", split_axis=0, concat_axis=0, tiled=True)
    arrived_counts = lax.all_to_all(
        counts[:, None], "expert", split_axis=0, concat_axis=0, tiled=True
    )[:, 0]
    offsets = jnp.cumsum(arrived_counts) - arrived_counts
    limit = capacity[0, 0]
    spare = jnp.maximum(limit - jnp.sum(arrived_counts), 0)
    pairs = [(source, source ^ (groups // 2)) for source in range(groups)]
    partner_spare = lax.ppermute(spare[None], "dp", pairs)[0]
    total_limit = limit + jnp.minimum(BLOCK, partner_spare)
    kept = jnp.clip(total_limit - offsets, 0, arrived_counts)
    keep = (slot_ids[None, :] < kept[:, None]).reshape(-1)
    rows = arrived.reshape(experts * SLOT, width)
    gated = jnp.dot(rows, w_gate[0], preferred_element_type=jnp.float32)
    upward = jnp.dot(rows, w_up[0], preferred_element_type=jnp.float32)
    hidden = (jax.nn.silu(gated) * upward).astype(jnp.bfloat16)
    computed = jnp.dot(hidden, w_down[0], preferred_element_type=jnp.float32)
    answers = jnp.where(keep[:, None], computed, 0.0).astype(jnp.bfloat16)
    back = lax.all_to_all(
        answers.reshape(experts, SLOT, width), "expert", split_axis=0, concat_axis=0, tiled=True
    ).reshape(experts * SLOT, width)
    spread = (position[:, :, None] == slot_ids[None, None, :]) & chosen[:, :, None]
    combine = jnp.where(spread, weight[:, :, None], 0.0).reshape(-1, experts * SLOT)
    high = combine.astype(jnp.bfloat16)
    low = (combine - high.astype(jnp.float32)).astype(jnp.bfloat16)
    mixed = jnp.dot(high, back, preferred_element_type=jnp.float32) + jnp.dot(
        low, back, preferred_element_type=jnp.float32
    )
    return mixed.astype(jnp.bfloat16)


def solution(mesh):
    return jax.shard_map(
        on_device,
        mesh=mesh,
        in_specs=(
            P(("dp", "expert"), None),
            P(("dp", "expert"), None),
            P(("dp", "expert"), None),
            P("expert", None, None),
            P("expert", None, None),
            P("expert", None, None),
            P("dp", "expert"),
        ),
        out_specs=P(("dp", "expert"), None),
        check_vma=False,
    )
```

time: 246 us -> 165 us (0.67); the launches traced: 241 us -> 164 us
  waiting for transfers between devices: 123 us -> 94.7 us
  starting transfers between devices: 53.5 us -> 29.6 us
  local copies, waits for them, and re-layouts: 20.8 us -> 1.83 us
  other arithmetic: 13.8 us -> 2.3 us
  matrix products: 28.8 us -> 33.1 us
    ppermute x2 -> x1, waiting for transfers between devices: 20 us -> 0.02 us  [on_device(): partner_spare = lax.ppermute(spare[None], 'dp', pairs)[0]]
    all_to_all x1, starting transfers between devices: 26.6 us -> 7.3 us  [on_device(): lax.all_to_all(answers.reshape(experts, SLOT, width), 'expert', split_axi...]
    gather x1 -> x0, local copies, waits for them, and re-layouts: 19.1 us -> none  [on_device(): jnp.take(back.reshape(resident_experts * capacity_positions, width), flat...]
    reduce_sum x3 -> x2, other arithmetic: 11.6 us -> 1.22 us  [the longest x1 1.2 us: on_device(): spare = jnp.maximum(limit - jnp.sum(arrived_counts), 0)]
    all_to_all x1, waiting for transfers between devices: 49.7 us -> 41 us  [on_device(): lax.all_to_all(send_rows, 'expert', split_axis=0, concat_axis=0, tiled=True)]
    ppermute x2 -> x1, starting transfers between devices: 12.3 us -> 7.71 us  [on_device(): partner_spare = lax.ppermute(spare[None], 'dp', pairs)[0]]
    dot_general x5 -> x4, matrix products: 24.3 us -> 28.7 us  [the longest x1 12.3 us: on_device(): computed = jnp.dot(hidden, w_down[0], preferred_element_type=jnp.float32)]
  transfers between devices with their start and end apart: 5 -> 4, of which waited for: 5 -> 3; matrix products, arithmetic and copies ran while one was open for 3% -> 4% of each run, Pallas kernels for 0% -> 0%
where the time goes in v1:
time: 165 us; the launch traced here: 164 us
  waiting for transfers between devices  94.7 us (57%)
  matrix products  33.1 us (20%)
  starting transfers between devices  29.6 us (18%)
  other arithmetic  2.3 us (1%)
  between operations  2.01 us (1%)
  local copies, waits for them, and re-layouts  1.83 us (1%)
    all_to_all x1, waiting for transfers between devices, on_device(): lax.all_to_all(answers.reshape(experts, SLOT, width), 'expert', split_axi...  52.2 us
    all_to_all x1, waiting for transfers between devices, on_device(): lax.all_to_all(send_rows, 'expert', split_axis=0, concat_axis=0, tiled=True)  41 us
    dot_general x1, matrix products, on_device(): computed = jnp.dot(hidden, w_down[0], preferred_element_type=jnp.float32)  12.3 us
    all_to_all x1, starting transfers between devices, on_device(): lax.all_to_all(counts[:, None], 'expert', split_axis=0, concat_axis=0, ti...  8.59 us
    dot_general x1, matrix products, on_device(): upward = jnp.dot(rows, w_up[0], preferred_element_type=jnp.float32)  8.33 us
    ppermute x1, starting transfers between devices, on_device(): partner_spare = lax.ppermute(spare[None], 'dp', pairs)[0]  7.71 us
    all_to_all x1, starting transfers between devices, on_device(): lax.all_to_all(answers.reshape(experts, SLOT, width), 'expert', split_axi...  7.3 us
    all_to_all x1, starting transfers between devices, on_device(): lax.all_to_all(send_rows, 'expert', split_axis=0, concat_axis=0, tiled=True)  5.96 us
  transfers between devices with their start and end apart: 4, of which 3 were waited for; matrix products, arithmetic and copies ran while one was open for 4% of the time, Pallas kernels for 0%

profile of v1, /device:TPU:1, one launch (start us, length us, event | category | flops | bytes accessed | tf_op | source)
XLA Modules:
  0.0 163.5 jit_solution(3123122912513454960)
XLA Ops:
  0.0 0.8 slice.12
  0.9 0.1 convert_reduce_fusion
  1.0 0.7 copy.30
  1.7 8.6 %all-to-all-start = ((s32[32,1,1]{2,1,0:T(1,128)}), s32[32,1,1]{2,1,0:T(1,128)S(1)}, u32[]{:S(2)}, u32[]{:S(2)}) async-start(s32[32,1,1]{2,1,0:T(1,128)} %copy.30), calls=%async_computation | async-start | bytes 32768 | tf_op jit(solution)/shard_map/all_to_all | solution.py:28
  10.3 0.6 reduce-window.18
  10.9 0.2 slice_reduce_fusion
  11.1 0.1 fusion.31
  11.2 4.5 %convolution_convert_fusion = bf16[32,32,2048]{2,1,0:T(8,128)(2,1)} fusion(bf16[256,2048]{1,0:T(8,128)(2,1)} %param.7, s32[32,256]{1,0:T(8,128)S(1)} %get-tuple-element.8, pred[32,256]{1,0:T(8,128)(4,1)S(1)} %bitcast.56), kind=kOutput, calls=%fused_computation.1 | convolution fusion | flops 1076363264 | bytes 5283840 | tf_op jit(solution)/shard_map/jpt,td->jpd/dot_general | solution.py:24
  15.7 1.5 all-to-all-done
  17.1 6.0 %all-to-all-start.1 = ((bf16[32,32,2048]{2,1,0:T(8,128)(2,1)}), bf16[32,32,2048]{2,1,0:T(8,128)(2,1)}, u32[]{:S(2)}, u32[]{:S(2)}) async-start(bf16[32,32,2048]{2,1,0:T(8,128)(2,1)} %convolution_convert_fusion), calls=%async_computation.1 | async-start | bytes 8388608 | tf_op jit(solution)/shard_map/all_to_all | solution.py:27
  23.8 1.2 fusion.32
  25.6 7.7 %collective-permute-start = (s32[1]{0:T(128)}, s32[1]{0:T(128)}, u32[]{:S(2)}, u32[]{:S(2)}) collective-permute-start(s32[1]{0:T(128)} %bitcast.4), channel_id=1, source_target_pairs={{0,128},{32,160},{64,192},{96,224},{128,0},{160,32},{192,64},{224,... | collective-permute-start | bytes 20 | tf_op jit(solution)/shard_map/ppermute | solution.py:35
  33.3 0.1 reduce-window.20
  33.4 0.1 reduce.4
  33.5 0.0 collective-permute-done
  34.2 0.1 iota_compare_fusion.3
  34.2 0.1 lt.23
  34.3 41.0 %all-to-all-done.1 = bf16[32,32,2048]{2,1,0:T(8,128)(2,1)} async-done(((bf16[32,32,2048]{2,1,0:T(8,128)(2,1)}), bf16[32,32,2048]{2,1,0:T(8,128)(2,1)}, u32[]{:S(2)}, u32[]{:S(2)}) %all-to-all-start.1) | async-done | bytes 4194336 | tf_op jit(solution)/shard_map/all_to_all | solution.py:27
  75.3 8.3 %fusion.1 = f32[1024,768]{1,0:T(8,128)} fusion(bf16[1024,2048]{1,0:T(8,128)(2,1)} %bitcast.8, bf16[1,2048,768]{2,1,0:T(8,128)(2,1)} %param.11), kind=kOutput, calls=%fused_computation.3 | convolution fusion | flops 3221225472 | bytes 10485760 | tf_op jit(solution)/shard_map/dot_general | solution.py:41
  83.7 12.3 %select_convert_fusion = bf16[1024,2048]{1,0:T(8,128)(2,1)} fusion(pred[1024]{0:T(1024)(128)(4,1)S(1)} %lt.23, bf16[1,768,2048]{2,1,0:T(8,128)(2,1)S(1)} %copy-done, f32[1024,768]{1,0:T(8,128)} %fusion.1, bf16[1024,2048]{1,0:T(8,128)(2,1)} %bitcast.8, bf16[1,2048,768]{2,1,0:T(8,128)(2,1)} %param.10), kind=kOutput, calls=%fused_computation | convolution fusion | flops 6451363840 | bytes 17826816 | tf_op jit(solution)/shard_map/dot_general | solution.py:43
  96.0 7.3 %all-to-all-start.2 = ((bf16[32,32,2048]{2,1,0:T(8,128)(2,1)}), bf16[32,32,2048]{2,1,0:T(8,128)(2,1)}, u32[]{:S(2)}, u32[]{:S(2)}) async-start(bf16[32,32,2048]{2,1,0:T(8,128)(2,1)} %bitcast.54), calls=%async_computation.2 | async-start | bytes 8388608 | tf_op jit(solution)/shard_map/all_to_all | solution.py:45
  103.3 52.2 %all-to-all-done.2 = bf16[32,32,2048]{2,1,0:T(8,128)(2,1)} async-done(((bf16[32,32,2048]{2,1,0:T(8,128)(2,1)}), bf16[32,32,2048]{2,1,0:T(8,128)(2,1)}, u32[]{:S(2)}, u32[]{:S(2)}) %all-to-all-start.2) | async-done | bytes 4194336 | tf_op jit(solution)/shard_map/all_to_all | solution.py:45
  155.5 3.5 %convolution_bitcast_fusion = f32[256,2048]{1,0:T(8,128)S(1)} fusion(bf16[32,32,2048]{2,1,0:T(8,128)(2,1)} %all-to-all-done.2, f32[256,32]{0,1:T(8,128)S(1)} %select_reduce_fusion, s32[256,32]{0,1:T(8,128)S(1)} %get-tuple-element.7, pred[256,32]{0,1:T(8,128)(4,1)S(1)} %fusion.27), kind=kOutput, calls=%fused_computation.8 | convolution fusion | flops 1075576832 | bytes 6365184 | tf_op jit(solution)/shard_map/dot_general | solution.py:52
  159.0 4.5 %fusion.6 = bf16[256,2048]{1,0:T(8,128)(2,1)} fusion(f32[256,2048]{1,0:T(8,128)S(1)} %convolution_bitcast_fusion, bf16[32,32,2048]{2,1,0:T(8,128)(2,1)} %all-to-all-done.2, f32[256,32]{0,1:T(8,128)S(1)} %select_reduce_fusion, s32[256,32]{0,1:T(8,128)S(1)} %get-tuple-element.7, pred[256,32]{0,1:T(8,128)(4,1)S(1)} %fusion.27), kind=kOutput, calls=%fused_computation.11 | convolution fusion | flops 1075576832 | bytes 7413760 | tf_op jit(solution)/shard_map/dot_general | solution.py:52
  (10 shorter events, 0.1 us)
Async XLA Ops:
  0.0 83.7 %copy-start = (bf16[1,768,2048]{2,1,0:T(8,128)(2,1)S(1)}, bf16[1,768,2048]{2,1,0:T(8,128)(2,1)}, u32[]{:S(2)}) copy-start(bf16[1,768,2048]{2,1,0:T(8,128)(2,1)} %param.12) | copy-start | bytes 9437188
  1.7 15.5 %all-to-all-start = ((s32[32,1,1]{2,1,0:T(1,128)}), s32[32,1,1]{2,1,0:T(1,128)S(1)}, u32[]{:S(2)}, u32[]{:S(2)}) async-start(s32[32,1,1]{2,1,0:T(1,128)} %copy.30), calls=%async_computation | async-start | bytes 32768 | tf_op jit(solution)/shard_map/all_to_all | solution.py:28
  17.1 58.2 %all-to-all-start.1 = ((bf16[32,32,2048]{2,1,0:T(8,128)(2,1)}), bf16[32,32,2048]{2,1,0:T(8,128)(2,1)}, u32[]{:S(2)}, u32[]{:S(2)}) async-start(bf16[32,32,2048]{2,1,0:T(8,128)(2,1)} %convolution_convert_fusion), calls=%async_computation.1 | async-start | bytes 8388608 | tf_op jit(solution)/shard_map/all_to_all | solution.py:27
  25.6 7.9 %collective-permute-start = (s32[1]{0:T(128)}, s32[1]{0:T(128)}, u32[]{:S(2)}, u32[]{:S(2)}) collective-permute-start(s32[1]{0:T(128)} %bitcast.4), channel_id=1, source_target_pairs={{0,128},{32,160},{64,192},{96,224},{128,0},{160,32},{192,64},{224,... | collective-permute-start | bytes 20 | tf_op jit(solution)/shard_map/ppermute | solution.py:35
  96.0 7.3 %slice-start = ((f32[256,8]{0,1:T(8,128)}), f32[256,2]{0,1:T(2,128)S(1)}, s32[]{:S(2)}) async-start(f32[256,8]{0,1:T(8,128)} %param.9), calls=%async_computation.3 | async-start | bytes 4096 | tf_op jit(solution)/shard_map/slice | solution.py:18
  96.0 59.5 %all-to-all-start.2 = ((bf16[32,32,2048]{2,1,0:T(8,128)(2,1)}), bf16[32,32,2048]{2,1,0:T(8,128)(2,1)}, u32[]{:S(2)}, u32[]{:S(2)}) async-start(bf16[32,32,2048]{2,1,0:T(8,128)(2,1)} %bitcast.54), calls=%async_computation.2 | async-start | bytes 8388608 | tf_op jit(solution)/shard_map/all_to_all | solution.py:45

commit v2 on v1

v2 whole, which is shorter than its diff:
```python
import functools
import jax
import jax.numpy as jnp
from jax import lax
from jax.experimental import pallas as pl
from jax.experimental.pallas import tpu as pltpu
from jax.sharding import PartitionSpec as P

BLOCK = 128
SLOT = 32
EXPERTS = 32
PART = 8
ROWS = PART * SLOT
PARTS = EXPERTS // PART
MESH = pl.DeviceIdType.MESH
F32 = jnp.float32
BF16 = jnp.bfloat16


def step_of(r):
    dx = (r % PART) // 2
    return dx, (r // PART + dx) % 4, r % 2


def target(me, r):
    dx, dy, dc = step_of(r)
    x, y, c = me // 8, (me // 2) % 4, me % 2
    return ((x + dx) % 4) * 8 + ((y + dy) % 4) * 2 + (c + dc) % 2


def origin(me, r):
    dx, dy, dc = step_of(r)
    x, y, c = me // 8, (me // 2) % 4, me % 2
    return ((x + 4 - dx) % 4) * 8 + ((y + 4 - dy) % 4) * 2 + (c + dc) % 2


def iota(shape, axis):
    return lax.broadcasted_iota(jnp.int32, shape, axis)


def kernel(
    tokens_hbm, index_ref, gate_ref, w_gate_hbm, w_up_hbm, w_down_hbm, capacity_ref,
    mixed_ref,
    tok, w_gate, w_up, w_down, send, recv, answer, back, spot, scaled, hidden, total,
    count_out, count_in, spare_out, spare_in,
    load_sem, send_sem, recv_sem, ret_send, ret_recv, cnt_send, cnt_recv, spare_sem,
):
    me = lax.axis_index("expert")
    group = lax.axis_index("dp")
    groups = lax.axis_size("dp")
    partner = (group + groups // 2) % groups

    loads = [
        pltpu.make_async_copy(src, dst, load_sem.at[i])
        for i, (src, dst) in enumerate(
            [
                (tokens_hbm, tok),
                (w_gate_hbm.at[0], w_gate),
                (w_up_hbm.at[0], w_up),
                (w_down_hbm.at[0], w_down),
            ]
        )
    ]
    for load in loads:
        load.start()

    barrier = pltpu.get_barrier_semaphore()

    @pl.loop(1, EXPERTS)
    def _(r):
        pl.semaphore_signal(barrier, inc=1, device_id=(group, target(me, r)), device_id_type=MESH)

    pl.semaphore_signal(barrier, inc=1, device_id=(partner, me), device_id_type=MESH)

    index = index_ref[...]
    experts = iota((EXPERTS, 256), 0)
    named = (experts == index[0:1, :]) | (experts == index[1:2, :])
    named_f = named.astype(F32)
    earlier = (iota((256, 256), 0) < iota((256, 256), 1)).astype(BF16)
    place = jnp.dot(named_f.astype(BF16), earlier, preferred_element_type=F32)
    spot[...] = jnp.where(named, place, -1.0)
    counts = jnp.dot(named_f.astype(BF16), jnp.ones((256, 128), BF16), preferred_element_type=F32)
    repeat = (iota((8 * EXPERTS, EXPERTS), 0) // 8 == iota((8 * EXPERTS, EXPERTS), 1)).astype(BF16)
    count_out[...] = jnp.dot(repeat, counts.astype(BF16), preferred_element_type=F32)
    count_in[pl.ds(0, 8), :] = count_out[pl.ds(pl.multiple_of(me * 8, 8), 8), :]

    pl.semaphore_wait(barrier, EXPERTS)

    def count_copy(r):
        to = target(me, r)
        return pltpu.make_async_remote_copy(
            src_ref=count_out.at[pl.ds(pl.multiple_of(to * 8, 8), 8), :],
            dst_ref=count_in.at[pl.ds(pl.multiple_of(r * 8, 8), 8), :],
            send_sem=cnt_send.at[r],
            recv_sem=cnt_recv.at[r],
            device_id=(group, to),
            device_id_type=MESH,
        )

    def row_copy(r):
        rows = pl.ds(pl.multiple_of(r * SLOT, SLOT), SLOT)
        return pltpu.make_async_remote_copy(
            src_ref=send.at[rows, :],
            dst_ref=recv.at[rows, :],
            send_sem=send_sem.at[r],
            recv_sem=recv_sem.at[r],
            device_id=(group, target(me, r)),
            device_id_type=MESH,
        )

    def answer_copy(r):
        rows = pl.ds(pl.multiple_of(r * SLOT, SLOT), SLOT)
        return pltpu.make_async_remote_copy(
            src_ref=answer.at[rows, :],
            dst_ref=back.at[rows, :],
            send_sem=ret_send.at[r],
            recv_sem=ret_recv.at[r],
            device_id=(group, origin(me, r)),
            device_id_type=MESH,
        )

    spare_copy = pltpu.make_async_remote_copy(
        src_ref=spare_out,
        dst_ref=spare_in,
        send_sem=spare_sem.at[0],
        recv_sem=spare_sem.at[1],
        device_id=(partner, me),
        device_id_type=MESH,
    )

    @pl.loop(1, EXPERTS)
    def _(r):
        count_copy(r).start()

    loads[0].wait()
    slot_id = iota((SLOT, 256), 0).astype(F32)

    @pl.loop(0, PARTS)
    def _(b):
        blocks = []
        for j in range(PART):
            line = spot[pl.ds(target(me, b * PART + j), 1), :]
            blocks.append((line == slot_id).astype(F32))
        placer = jnp.concatenate(blocks, axis=0).astype(BF16)
        rows = pl.ds(pl.multiple_of(b * ROWS, ROWS), ROWS)
        send[rows, :] = jnp.dot(placer, tok[...], preferred_element_type=F32).astype(BF16)

        @pl.when(b == 0)
        def _():
            recv[pl.ds(0, SLOT), :] = send[pl.ds(0, SLOT), :]

        @pl.loop(0, PART)
        def _(j):
            @pl.when(b * PART + j > 0)
            def _():
                row_copy(b * PART + j).start()

    @pl.loop(0, EXPERTS)
    def _(r):
        to = target(me, r)
        line = spot[pl.ds(to, 1), :]
        weight = gate_ref[pl.ds(to // 16, 1), :]
        rows = pl.ds(pl.multiple_of(r * SLOT, SLOT), SLOT)
        scaled[rows, :] = jnp.where(line == slot_id, weight, 0.0).astype(BF16)

    @pl.loop(1, EXPERTS)
    def _(r):
        count_copy(r).wait_recv()

    arrived = count_in[...].astype(BF16)
    r_row = iota((EXPERTS, 8 * EXPERTS), 0)
    r_col = iota((EXPERTS, 8 * EXPERTS), 1)
    pick = (r_col == 8 * r_row).astype(BF16)
    before = (
        (r_col % 8 == 0) & (origin(me, r_col // 8) < origin(me, r_row))
    ).astype(BF16)
    count = jnp.dot(pick, arrived, preferred_element_type=F32)
    offset = jnp.dot(before, arrived, preferred_element_type=F32)
    limit = capacity_ref[0, 0].astype(F32)
    spare = jnp.maximum(limit - jnp.sum(count, axis=0, keepdims=True), 0.0)
    spare_out[...] = jnp.broadcast_to(spare, (8, 128))
    spare_copy.start()
    spare_copy.wait_recv()
    room = limit + jnp.minimum(spare_in[0:1, :], float(BLOCK))
    kept = jnp.minimum(jnp.maximum(room - offset, 0.0), count).astype(BF16)

    for load in loads[1:]:
        load.wait()

    @pl.loop(0, PARTS)
    def _(b):
        @pl.loop(0, PART)
        def _(j):
            @pl.when(b * PART + j > 0)
            def _():
                row_copy(b * PART + j).wait_recv()

        rows = pl.ds(pl.multiple_of(b * ROWS, ROWS), ROWS)
        own = (iota((ROWS, EXPERTS), 0) // SLOT + b * PART == iota((ROWS, EXPERTS), 1)).astype(BF16)
        most = jnp.dot(own, kept, preferred_element_type=F32)[:, 0:1]
        keep = (iota((ROWS, 1), 0) % SLOT).astype(F32) < most
        x = recv[rows, :]
        for f in range(3):
            cols = pl.ds(f * 256, 256)
            gated = jnp.dot(x, w_gate[:, cols], preferred_element_type=F32)
            upward = jnp.dot(x, w_up[:, cols], preferred_element_type=F32)
            value = gated / (1.0 + jnp.exp(-gated)) * upward
            hidden[:, cols] = jnp.where(keep, value, 0.0).astype(BF16)
        h = hidden[...]
        for d in range(4):
            cols = pl.ds(d * 512, 512)
            answer[rows, cols] = jnp.dot(
                h, w_down[:, cols], preferred_element_type=F32
            ).astype(BF16)

        @pl.when(b == 0)
        def _():
            back[pl.ds(0, SLOT), :] = answer[pl.ds(0, SLOT), :]

        @pl.loop(0, PART)
        def _(j):
            @pl.when(b * PART + j > 0)
            def _():
                answer_copy(b * PART + j).start()

    total[...] = jnp.zeros_like(total)

    @pl.loop(0, PARTS)
    def _(b):
        @pl.loop(0, PART)
        def _(j):
            @pl.when(b * PART + j > 0)
            def _():
                answer_copy(b * PART + j).wait_recv()

        rows = pl.ds(pl.multiple_of(b * ROWS, ROWS), ROWS)
        total[...] += lax.dot_general(
            scaled[rows, :], back[rows, :], (((0,), (0,)), ((), ())), preferred_element_type=F32
        )

    mixed_ref[...] = total[...].astype(BF16)

    @pl.loop(1, EXPERTS)
    def _(r):
        count_copy(r).wait_send()
        row_copy(r).wait_send()
        answer_copy(r).wait_send()

    spare_copy.wait_send()


def on_device(tokens, chosen_expert_index, routing_gate_weight, w_gate, w_up, w_down, capacity):
    rows, width = tokens.shape
    units = w_gate.shape[2]
    total_rows = EXPERTS * SLOT
    hbm = pl.BlockSpec(memory_space=pl.ANY)
    vmem = pl.BlockSpec(memory_space=pltpu.VMEM)
    smem = pl.BlockSpec(memory_space=pltpu.SMEM)
    dma = pltpu.SemaphoreType.DMA
    return pl.pallas_call(
        kernel,
        out_shape=jax.ShapeDtypeStruct((rows, width), BF16),
        in_specs=[hbm, vmem, vmem, hbm, hbm, hbm, smem],
        out_specs=vmem,
        scratch_shapes=[
            pltpu.VMEM((rows, width), BF16),
            pltpu.VMEM((width, units), BF16),
            pltpu.VMEM((width, units), BF16),
            pltpu.VMEM((units, width), BF16),
            pltpu.VMEM((total_rows, width), BF16),
            pltpu.VMEM((total_rows, width), BF16),
            pltpu.VMEM((total_rows, width), BF16),
            pltpu.VMEM((total_rows, width), BF16),
            pltpu.VMEM((EXPERTS, rows), F32),
            pltpu.VMEM((total_rows, rows), BF16),
            pltpu.VMEM((ROWS, units), BF16),
            pltpu.VMEM((rows, width), F32),
            pltpu.VMEM((8 * EXPERTS, 128), F32),
            pltpu.VMEM((8 * EXPERTS, 128), F32),
            pltpu.VMEM((8, 128), F32),
            pltpu.VMEM((8, 128), F32),
            dma((4,)),
            dma((EXPERTS,)),
            dma((EXPERTS,)),
            dma((EXPERTS,)),
            dma((EXPERTS,)),
            dma((EXPERTS,)),
            dma((EXPERTS,)),
            dma((2,)),
        ],
        compiler_params=pltpu.CompilerParams(
            collective_id=0, has_side_effects=True, vmem_limit_bytes=56 * 2**20
        ),
        cost_estimate=pl.CostEstimate(
            flops=6 * total_rows * width * units, bytes_accessed=6 * width * units, transcendentals=0
        ),
    )(
        tokens,
        chosen_expert_index[:, :8].T,
        routing_gate_weight[:, :8].T,
        w_gate,
        w_up,
        w_down,
        capacity,
    )


def solution(mesh):
    return jax.shard_map(
        on_device,
        mesh=mesh,
        in_specs=(
            P(("dp", "expert"), None),
            P(("dp", "expert"), None),
            P(("dp", "expert"), None),
            P("expert", None, None),
            P("expert", None, None),
            P("expert", None, None),
            P("dp", "expert"),
        ),
        out_specs=P(("dp", "expert"), None),
        check_vma=False,
    )
```

time: 165 us -> 145 us (0.88)
  the two profiles are of different devices: /device:TPU:1 before, /device:TPU:155 now
where the time goes in v2:
time: 145 us
  Pallas kernels  142 us (98%)
  local copies, waits for them, and re-layouts  2.3 us (2%)
    pallas_call x1, Pallas kernels, on_device(): pl.pallas_call(kernel, out_shape=jax.ShapeDtypeStruct((rows, width), BF16...  142 us

profile of v2, /device:TPU:155, one launch (start us, length us, event | category | flops | bytes accessed | tf_op | source)
XLA Modules:
  0.0 144.9 jit_solution(4835860012845800164)
XLA Ops:
  0.7 141.9 %shard_map.73 = bf16[256,2048]{1,0:T(8,128)(2,1)} custom-call(bf16[256,2048]{1,0:T(8,128)(2,1)} %tokens_hbm.1, s32[8,256]{1,0:T(8,128)} %bitcast.2, f32[8,256]{1,0:T(8,128)} %bitcast.3, bf16[1,2048,768]{2,1,0:T(8,128)(2,1)} %w_gate_hbm.1, bf16[1,2048,768]{2,1,0:T(8,128)(2,1)} %w_up_hbm.1, bf16[1,768,2048]{2,1,0:T(8,128)(2,1)} %w_down_hbm.1, ...), custom_call_target="tpu_custom_call" | custom-call | flops 9663676416 | bytes 9437184 | tf_op jit(solution)/shard_map/pallas_call | solution.py:260
  142.6 2.3 %copy.10 = bf16[256,2048]{1,0:T(8,128)(2,1)} copy(bf16[256,2048]{1,0:T(8,128)(2,1)} %shard_map.73) | data formatting | bytes 2097152

commit v3 on v1

v3 whole, which is shorter than its diff:
```python
import jax
import jax.numpy as jnp
from jax import lax
from jax.experimental import pallas as pl
from jax.experimental.pallas import tpu as pltpu
from jax.sharding import PartitionSpec as P

BLOCK = 128
SLOT = 32
EXPERTS = 32
SPLIT = 2
PIECE = SLOT // SPLIT
ROWS = 16 * PIECE
MESH = pl.DeviceIdType.MESH
F32 = jnp.float32
BF16 = jnp.bfloat16


def iota(shape, axis):
    return lax.broadcasted_iota(jnp.int32, shape, axis)


def kernel(
    tokens_hbm, index_ref, gate_ref, w_gate_hbm, w_up_hbm, w_down_hbm, capacity_ref,
    mixed_ref,
    tok, w_gate, w_up, w_down, send, relay_a, relay_b, recv, answer, home_a, home_b, back,
    spot, scaled, hidden, total, count_out, count_in, spare_out, spare_in,
    load_sem, local_sem, cnt_send, cnt_recv, spare_sem,
    a1_send, a1_recv, b1_send, b1_recv, a2_send, a2_recv, b2_send, b2_recv,
    c1_send, c1_recv, d1_send, d1_recv, c2_send, c2_recv, d2_send, d2_recv,
):
    me = lax.axis_index("expert")
    group = lax.axis_index("dp")
    groups = lax.axis_size("dp")
    partner = (group + groups // 2) % groups
    x, y, c = me // 8, (me // 2) % 4, me % 2
    half = tok.shape[1] // 2
    low, high = pl.ds(0, half), pl.ds(half, half)

    def remote(src, dst, sends, recvs, xd, yd, cd):
        return pltpu.make_async_remote_copy(
            src_ref=src,
            dst_ref=dst,
            send_sem=sends,
            recv_sem=recvs,
            device_id=(group, xd * 8 + yd * 2 + cd),
            device_id_type=MESH,
        )

    def a1(q, dx):
        xd = (x + dx) % 4
        return remote(
            send.at[q, xd, :, :, :, low], relay_a.at[q, :, :, x],
            a1_send.at[q, dx], a1_recv.at[q, dx], xd, y, c,
        )

    def b1(q, dy):
        yd = (y + dy) % 4
        return remote(
            send.at[q, :, yd, :, :, high], relay_b.at[q, :, :, y],
            b1_send.at[q, dy], b1_recv.at[q, dy], x, yd, c,
        )

    def a2(q, j):
        yd, cd = (y + j // 2) % 4, (c + j % 2) % 2
        return remote(
            relay_a.at[q, yd, cd], recv.at[q, c, y, :, :, low],
            a2_send.at[q, j], a2_recv.at[q, j], x, yd, cd,
        )

    def b2(q, j):
        xd, cd = (x + j // 2) % 4, (c + j % 2) % 2
        return remote(
            relay_b.at[q, xd, cd], recv.at[q, c, :, x, :, high],
            b2_send.at[q, j], b2_recv.at[q, j], xd, y, cd,
        )

    def c1(q, j):
        yd, cd = (y + j // 2) % 4, (c + j % 2) % 2
        return remote(
            answer.at[q, cd, yd, :, :, low], home_a.at[q, y, c],
            c1_send.at[q, j], c1_recv.at[q, j], x, yd, cd,
        )

    def d1(q, j):
        xd, cd = (x + j // 2) % 4, (c + j % 2) % 2
        return remote(
            answer.at[q, cd, :, xd, :, high], home_b.at[q, x, c],
            d1_send.at[q, j], d1_recv.at[q, j], xd, y, cd,
        )

    def c2(q, dx):
        xd = (x + dx) % 4
        return remote(
            home_a.at[q, :, :, xd], back.at[q, x, :, :, :, low],
            c2_send.at[q, dx], c2_recv.at[q, dx], xd, y, c,
        )

    def d2(q, dy):
        yd = (y + dy) % 4
        return remote(
            home_b.at[q, :, :, yd], back.at[q, :, y, :, :, high],
            d2_send.at[q, dy], d2_recv.at[q, dy], x, yd, c,
        )

    def own(q, hop):
        src, dst = [
            (send.at[q, x, :, :, :, low], relay_a.at[q, :, :, x]),
            (send.at[q, :, y, :, :, high], relay_b.at[q, :, :, y]),
            (relay_a.at[q, y, c], recv.at[q, c, y, :, :, low]),
            (relay_b.at[q, x, c], recv.at[q, c, :, x, :, high]),
            (answer.at[q, c, y, :, :, low], home_a.at[q, y, c]),
            (answer.at[q, c, :, x, :, high], home_b.at[q, x, c]),
            (home_a.at[q, :, :, x], back.at[q, x, :, :, :, low]),
            (home_b.at[q, :, :, y], back.at[q, :, y, :, :, high]),
        ][hop]
        return pltpu.make_async_copy(src, dst, local_sem.at[q, hop])

    def count_copy(r):
        to = (me + r) % EXPERTS
        return pltpu.make_async_remote_copy(
            src_ref=count_out.at[pl.ds(pl.multiple_of(to * 8, 8), 8), :],
            dst_ref=count_in.at[pl.ds(pl.multiple_of(me * 8, 8), 8), :],
            send_sem=cnt_send.at[r],
            recv_sem=cnt_recv.at[r],
            device_id=(group, to),
            device_id_type=MESH,
        )

    spare_copy = pltpu.make_async_remote_copy(
        src_ref=spare_out,
        dst_ref=spare_in,
        send_sem=spare_sem.at[0],
        recv_sem=spare_sem.at[1],
        device_id=(partner, me),
        device_id_type=MESH,
    )

    loads = [
        pltpu.make_async_copy(src, dst, load_sem.at[i])
        for i, (src, dst) in enumerate(
            [
                (tokens_hbm, tok),
                (w_gate_hbm.at[0], w_gate),
                (w_up_hbm.at[0], w_up),
                (w_down_hbm.at[0], w_down),
            ]
        )
    ]
    for load in loads:
        load.start()

    barrier = pltpu.get_barrier_semaphore()

    @pl.loop(1, EXPERTS)
    def _(r):
        pl.semaphore_signal(
            barrier, inc=1, device_id=(group, (me + r) % EXPERTS), device_id_type=MESH
        )

    pl.semaphore_signal(barrier, inc=1, device_id=(partner, me), device_id_type=MESH)

    index = index_ref[...]
    experts = iota((EXPERTS, 256), 0)
    named = (experts == index[0:1, :]) | (experts == index[1:2, :])
    named_b = named.astype(F32).astype(BF16)
    earlier = (iota((256, 256), 0) < iota((256, 256), 1)).astype(F32).astype(BF16)
    place = jnp.dot(named_b, earlier, preferred_element_type=F32)
    spot[...] = jnp.where(named, place, -1.0)
    counts = jnp.dot(named_b, jnp.ones((256, 128), BF16), preferred_element_type=F32)
    repeat = iota((8 * EXPERTS, EXPERTS), 0) // 8 == iota((8 * EXPERTS, EXPERTS), 1)
    count_out[...] = jnp.dot(
        repeat.astype(F32).astype(BF16), counts.astype(BF16), preferred_element_type=F32
    )
    mine = pl.ds(pl.multiple_of(me * 8, 8), 8)
    count_in[mine, :] = count_out[mine, :]
    loads[0].wait()

    piece_id = iota((PIECE, 256), 0)

    def pack(q):
        slot_id = (piece_id + q * PIECE).astype(F32)

        @pl.loop(0, 4)
        def _(xd):
            lines = spot[pl.ds(pl.multiple_of(xd * 8, 8), 8), :]
            placer = jnp.concatenate(
                [(lines[j : j + 1, :] == slot_id).astype(F32) for j in range(8)], axis=0
            )
            packed = jnp.dot(placer.astype(BF16), tok[...], preferred_element_type=F32)
            send[q, xd] = packed.astype(BF16).reshape(4, 2, PIECE, 2 * half)

    def start_first(q):
        @pl.loop(1, 4)
        def _(d):
            a1(q, d).start()
            b1(q, d).start()

        own(q, 0).start()
        own(q, 1).start()

    pack(0)
    pl.semaphore_wait(barrier, EXPERTS)

    @pl.loop(1, EXPERTS)
    def _(r):
        count_copy(r).start()

    start_first(0)
    pack(1)
    start_first(1)

    for q in range(SPLIT):
        slot_id = (piece_id + q * PIECE).astype(F32)

        @pl.loop(0, 4)
        def _(xd):
            lines = spot[pl.ds(pl.multiple_of(xd * 8, 8), 8), :]
            weight = gate_ref[pl.ds(xd // 2, 1), :]
            spread = jnp.concatenate(
                [jnp.where(lines[j : j + 1, :] == slot_id, weight, 0.0) for j in range(8)], axis=0
            )
            rows = pl.ds(pl.multiple_of(xd * 8 * PIECE, 8 * PIECE), 8 * PIECE)
            scaled[q, rows, :] = spread.astype(BF16)

    @pl.loop(1, EXPERTS)
    def _(r):
        count_copy(r).wait_recv()

    arrived = count_in[...].astype(BF16)
    row = iota((EXPERTS, 8 * EXPERTS), 0)
    col = iota((EXPERTS, 8 * EXPERTS), 1)
    pick = (col == 8 * row).astype(F32).astype(BF16)
    before = ((col % 8 == 0) & (col < 8 * row)).astype(F32).astype(BF16)
    count = jnp.dot(pick, arrived, preferred_element_type=F32)
    offset = jnp.dot(before, arrived, preferred_element_type=F32)
    limit = capacity_ref[0, 0].astype(F32)
    spare = jnp.maximum(limit - jnp.sum(count, axis=0, keepdims=True), 0.0)
    spare_out[...] = jnp.broadcast_to(spare, (8, 128))
    spare_copy.start()
    for q in range(SPLIT):

        @pl.loop(1, 4)
        def _(d):
            a1(q, d).wait_recv()
            b1(q, d).wait_recv()

        own(q, 0).wait()
        own(q, 1).wait()

        @pl.loop(0, 2)
        def _(dc):
            @pl.loop(0, 4)
            def _(d):
                @pl.when(d + dc > 0)
                def _():
                    a2(q, 2 * d + dc).start()
                    b2(q, 2 * d + dc).start()

        own(q, 2).start()
        own(q, 3).start()

    spare_copy.wait_recv()
    room = limit + jnp.minimum(spare_in[0:1, :], float(BLOCK))
    kept = jnp.minimum(jnp.maximum(room - offset, 0.0), count).astype(BF16)
    for load in loads[1:]:
        load.wait()

    for q in range(SPLIT):
        own(q, 2).wait()
        own(q, 3).wait()

        @pl.loop(0, 2)
        def _(dc):
            core = (c + dc) % 2

            @pl.loop(0, 4)
            def _(d):
                @pl.when(d + dc > 0)
                def _():
                    a2(q, 2 * d + dc).wait_recv()
                    b2(q, 2 * d + dc).wait_recv()

            place_id = iota((ROWS, EXPERTS), 0)
            source = (place_id // PIECE % 4) * 8 + (place_id // (4 * PIECE)) * 2 + core
            pick = (source == iota((ROWS, EXPERTS), 1)).astype(F32).astype(BF16)
            most = jnp.dot(pick, kept, preferred_element_type=F32)[:, 0:1]
            keep = (iota((ROWS, 1), 0) % PIECE + q * PIECE).astype(F32) < most
            rows = recv[q, core].reshape(ROWS, 2 * half)
            for f in range(3):
                cols = pl.ds(f * 256, 256)
                gated = jnp.dot(rows, w_gate[:, cols], preferred_element_type=F32)
                upward = jnp.dot(rows, w_up[:, cols], preferred_element_type=F32)
                value = gated / (1.0 + jnp.exp(-gated)) * upward
                hidden[:, cols] = jnp.where(keep, value, 0.0).astype(BF16)
            h = hidden[...]
            for d in range(4):
                cols = pl.ds(d * 512, 512)
                result = jnp.dot(h, w_down[:, cols], preferred_element_type=F32)
                answer[q, core, :, :, :, cols] = result.astype(BF16).reshape(4, 4, PIECE, 512)

            @pl.loop(0, 4)
            def _(d):
                @pl.when(d + dc > 0)
                def _():
                    c1(q, 2 * d + dc).start()
                    d1(q, 2 * d + dc).start()

        own(q, 4).start()
        own(q, 5).start()

    for q in range(SPLIT):

        @pl.loop(1, 8)
        def _(j):
            c1(q, j).wait_recv()
            d1(q, j).wait_recv()

        own(q, 4).wait()
        own(q, 5).wait()

        @pl.loop(1, 4)
        def _(d):
            c2(q, d).start()
            d2(q, d).start()

        own(q, 6).start()
        own(q, 7).start()

    for q in range(SPLIT):

        @pl.loop(1, 4)
        def _(d):
            c2(q, d).wait_recv()
            d2(q, d).wait_recv()

        own(q, 6).wait()
        own(q, 7).wait()
        part = lax.dot_general(
            scaled[q],
            back[q].reshape(EXPERTS * PIECE, 2 * half),
            (((0,), (0,)), ((), ())),
            preferred_element_type=F32,
        )
        if q == 0:
            total[...] = part
        else:
            mixed_ref[...] = (total[...] + part).astype(BF16)

    @pl.loop(1, EXPERTS)
    def _(r):
        count_copy(r).wait_send()

    spare_copy.wait_send()
    for q in range(SPLIT):

        @pl.loop(1, 4)
        def _(d):
            a1(q, d).wait_send()
            b1(q, d).wait_send()
            c2(q, d).wait_send()
            d2(q, d).wait_send()

        @pl.loop(1, 8)
        def _(j):
            a2(q, j).wait_send()
            b2(q, j).wait_send()
            c1(q, j).wait_send()
            d1(q, j).wait_send()


def on_device(tokens, chosen_expert_index, routing_gate_weight, w_gate, w_up, w_down, capacity):
    rows, width = tokens.shape
    units = w_gate.shape[2]
    half = width // 2
    hbm = pl.BlockSpec(memory_space=pl.ANY)
    vmem = pl.BlockSpec(memory_space=pltpu.VMEM)
    smem = pl.BlockSpec(memory_space=pltpu.SMEM)
    dma = pltpu.SemaphoreType.DMA
    wide = pltpu.VMEM((SPLIT, 4, 4, 2, PIECE, width), BF16)
    by_source = pltpu.VMEM((SPLIT, 2, 4, 4, PIECE, width), BF16)
    relay = pltpu.VMEM((SPLIT, 4, 2, 4, PIECE, half), BF16)
    near, far = dma((SPLIT, 4)), dma((SPLIT, 8))
    return pl.pallas_call(
        kernel,
        out_shape=jax.ShapeDtypeStruct((rows, width), BF16),
        in_specs=[hbm, vmem, vmem, hbm, hbm, hbm, smem],
        out_specs=vmem,
        scratch_shapes=[
            pltpu.VMEM((rows, width), BF16),
            pltpu.VMEM((width, units), BF16),
            pltpu.VMEM((width, units), BF16),
            pltpu.VMEM((units, width), BF16),
            wide,
            relay,
            relay,
            by_source,
            by_source,
            relay,
            relay,
            wide,
            pltpu.VMEM((EXPERTS, rows), F32),
            pltpu.VMEM((SPLIT, EXPERTS * PIECE, rows), BF16),
            pltpu.VMEM((ROWS, units), BF16),
            pltpu.VMEM((rows, width), F32),
            pltpu.VMEM((8 * EXPERTS, 128), F32),
            pltpu.VMEM((8 * EXPERTS, 128), F32),
            pltpu.VMEM((8, 128), F32),
            pltpu.VMEM((8, 128), F32),
            dma((4,)),
            dma((SPLIT, 8)),
            dma((EXPERTS,)),
            dma((EXPERTS,)),
            dma((2,)),
            near, near, near, near, far, far, far, far,
            far, far, far, far, near, near, near, near,
        ],
        compiler_params=pltpu.CompilerParams(
            collective_id=0, has_side_effects=True, vmem_limit_bytes=60 * 2**20
        ),
        cost_estimate=pl.CostEstimate(
            flops=6 * EXPERTS * SLOT * width * units,
            bytes_accessed=6 * width * units,
            transcendentals=0,
        ),
    )(
        tokens,
        chosen_expert_index[:, :8].T,
        routing_gate_weight[:, :8].T,
        w_gate,
        w_up,
        w_down,
        capacity,
    )


def solution(mesh):
    return jax.shard_map(
        on_device,
        mesh=mesh,
        in_specs=(
            P(("dp", "expert"), None),
            P(("dp", "expert"), None),
            P(("dp", "expert"), None),
            P("expert", None, None),
            P("expert", None, None),
            P("expert", None, None),
            P("dp", "expert"),
        ),
        out_specs=P(("dp", "expert"), None),
        check_vma=False,
    )
```

time: 165 us -> 112 us (0.68)
  Pallas kernels: 0 us -> 108 us
  waiting for transfers between devices: 94.7 us -> 0 us
  matrix products: 33.1 us -> 0 us
  starting transfers between devices: 29.6 us -> 0 us
  other arithmetic: 2.3 us -> 0 us
    pallas_call x0 -> x1, Pallas kernels: none -> 108 us  [on_device(): pl.pallas_call(kernel, out_shape=jax.ShapeDtypeStruct((rows, width), BF16...]
    all_to_all x3 -> x0, waiting for transfers between devices: 94.7 us -> none  [the longest x1 52.2 us: on_device(): lax.all_to_all(answers.reshape(experts, SLOT, width), 'expert', split_axi...]
    dot_general x5 -> x0, matrix products: 33.1 us -> none  [the longest x1 12.3 us: on_device(): computed = jnp.dot(hidden, w_down[0], preferred_element_type=jnp.float32)]
    all_to_all x3 -> x0, starting transfers between devices: 21.8 us -> none  [the longest x1 8.59 us: on_device(): lax.all_to_all(counts[:, None], 'expert', split_axis=0, concat_axis=0, ti...]
    ppermute x1 -> x0, starting transfers between devices: 7.71 us -> none  [on_device(): partner_spare = lax.ppermute(spare[None], 'dp', pairs)[0]]
    unnamed x2 -> x1, local copies, waits for them, and re-layouts: 0.01 us -> 2.3 us
  transfers between devices with their start and end apart: 4 -> 0, of which waited for: 3 -> 0; matrix products, arithmetic and copies ran while one was open for 4% -> 0% of each run, Pallas kernels for 0% -> 0%
where the time goes in v3:
time: 112 us; the launch traced here: 111 us
  Pallas kernels  108 us (96%)
  local copies, waits for them, and re-layouts  2.3 us (2%)
    pallas_call x1, Pallas kernels, on_device(): pl.pallas_call(kernel, out_shape=jax.ShapeDtypeStruct((rows, width), BF16...  108 us
    unnamed x1, local copies, waits for them, and re-layouts  2.3 us

profile of v3, /device:TPU:1, one launch (start us, length us, event | category | flops | bytes accessed | tf_op | source)
XLA Modules:
  0.0 111.1 jit_solution(2297452057228727312)
XLA Ops:
  0.7 108.1 %shard_map.73 = bf16[256,2048]{1,0:T(8,128)(2,1)} custom-call(bf16[256,2048]{1,0:T(8,128)(2,1)} %tokens_hbm.1, s32[8,256]{1,0:T(8,128)} %bitcast.2, f32[8,256]{1,0:T(8,128)} %bitcast.3, bf16[1,2048,768]{2,1,0:T(8,128)(2,1)} %w_gate_hbm.1, bf16[1,2048,768]{2,1,0:T(8,128)(2,1)} %w_up_hbm.1, bf16[1,768,2048]{2,1,0:T(8,128)(2,1)} %w_down_hbm.1, ...), custom_call_target="tpu_custom_call" | custom-call | flops 9663676416 | bytes 9437184 | tf_op jit(solution)/shard_map/pallas_call | solution.py:384
  108.8 2.3 %copy.10 = bf16[256,2048]{1,0:T(8,128)(2,1)} copy(bf16[256,2048]{1,0:T(8,128)(2,1)} %shard_map.73) | data formatting | bytes 2097152

commit v4 on v3

v4 whole, which is shorter than its diff:
```python
import jax
import jax.numpy as jnp
from jax import lax
from jax.experimental import pallas as pl
from jax.experimental.pallas import tpu as pltpu
from jax.sharding import PartitionSpec as P

BLOCK = 128
SLOT = 32
EXPERTS = 32
SPLIT = 2
PIECE = SLOT // SPLIT
ROWS = 16 * PIECE
MESH = pl.DeviceIdType.MESH
F32 = jnp.float32
BF16 = jnp.bfloat16


def iota(shape, axis):
    return lax.broadcasted_iota(jnp.int32, shape, axis)


def kernel(
    tokens_hbm, index_ref, gate_ref, w_gate_hbm, w_up_hbm, w_down_hbm, capacity_ref,
    mixed_ref,
    tok, w_gate, w_up, w_down, send, relay_a, relay_b, recv, answer, home_a, home_b, back,
    spot, scaled, hidden, total, count_out, count_relay, count_in, spare_out, spare_mid, spare_in,
    load_sem, local_sem, cnt_sem, spare_sem, near_send, near_recv, far_send, far_recv, ret_recv,
):
    me = lax.axis_index("expert")
    group = lax.axis_index("dp")
    groups = lax.axis_size("dp")
    stride = groups // 4
    x, y, c = me // 8, (me // 2) % 4, me % 2
    half = tok.shape[1] // 2
    low, high = pl.ds(0, half), pl.ds(half, half)

    def remote(src, dst, sends, recvs, xd, yd, cd):
        return pltpu.make_async_remote_copy(
            src_ref=src,
            dst_ref=dst,
            send_sem=sends,
            recv_sem=recvs,
            device_id=(group, xd * 8 + yd * 2 + cd),
            device_id_type=MESH,
        )

    def several(ref, sem):
        return remote(ref, ref, sem, sem, x, y, 1 - c)

    def a1(q, dx):
        xd = (x + dx) % 4
        return remote(
            send.at[q, xd, :, :, low], relay_a.at[q, :, x],
            near_send.at[0], near_recv.at[0, q], xd, y, c,
        )

    def b1(q, dy):
        yd = (y + dy) % 4
        return remote(
            send.at[q, :, pl.ds(yd * 2, 2), :, high], relay_b.at[q, :, :, y],
            near_send.at[1], near_recv.at[1, q], x, yd, c,
        )

    def a2(q, d, dc):
        yd, cd = (y + d) % 4, (c + dc) % 2
        return remote(
            relay_a.at[q, yd * 2 + cd], recv.at[q, c, y, :, :, low],
            far_send.at[0], far_recv.at[0, q, dc], x, yd, cd,
        )

    def b2(q, d, dc):
        xd, cd = (x + d) % 4, (c + dc) % 2
        return remote(
            relay_b.at[q, xd, cd], recv.at[q, c, :, x, :, high],
            far_send.at[1], far_recv.at[1, q, dc], xd, y, cd,
        )

    def c1(q, d, dc):
        yd, cd = (y + d) % 4, (c + dc) % 2
        return remote(
            answer.at[q, cd, yd, :, :, low], home_a.at[q, y * 2 + c],
            far_send.at[2], ret_recv.at[0, q], x, yd, cd,
        )

    def d1(q, d, dc):
        xd, cd = (x + d) % 4, (c + dc) % 2
        return remote(
            answer.at[q, cd, :, xd, :, high], home_b.at[q, x, c],
            far_send.at[3], ret_recv.at[1, q], xd, y, cd,
        )

    def c2(q, dx):
        xd = (x + dx) % 4
        return remote(
            home_a.at[q, :, xd], back.at[q, x, :, :, low],
            near_send.at[2], near_recv.at[2, q], xd, y, c,
        )

    def d2(q, dy):
        yd = (y + dy) % 4
        return remote(
            home_b.at[q, :, :, yd], back.at[q, :, pl.ds(y * 2, 2), :, high],
            near_send.at[3], near_recv.at[3, q], x, yd, c,
        )

    def own(q, hop):
        src, dst = [
            (send.at[q, x, :, :, low], relay_a.at[q, :, x]),
            (send.at[q, :, pl.ds(y * 2, 2), :, high], relay_b.at[q, :, :, y]),
            (relay_a.at[q, y * 2 + c], recv.at[q, c, y, :, :, low]),
            (relay_b.at[q, x, c], recv.at[q, c, :, x, :, high]),
            (answer.at[q, c, y, :, :, low], home_a.at[q, y * 2 + c]),
            (answer.at[q, c, :, x, :, high], home_b.at[q, x, c]),
            (home_a.at[q, :, x], back.at[q, x, :, :, low]),
            (home_b.at[q, :, :, y], back.at[q, :, pl.ds(y * 2, 2), :, high]),
        ][hop]
        return pltpu.make_async_copy(src, dst, local_sem.at[q, hop])

    def count_near(dx):
        xd = (x + dx) % 4
        return remote(
            count_out.at[pl.ds(pl.multiple_of(xd * 8, 8), 8), :], count_relay.at[x],
            cnt_sem.at[0], cnt_sem.at[1], xd, y, c,
        )

    def count_far(j):
        return remote(
            count_relay, count_in.at[c * 4 + y],
            cnt_sem.at[2], cnt_sem.at[3], x, (y + j // 2) % 4, (c + j % 2) % 2,
        )

    def spare_copy(hop):
        src, dst = [(spare_out, spare_mid), (spare_mid, spare_in)][hop]
        return pltpu.make_async_remote_copy(
            src_ref=src,
            dst_ref=dst,
            send_sem=spare_sem.at[hop],
            recv_sem=spare_sem.at[2 + hop],
            device_id=((group + stride) % groups, me),
            device_id_type=MESH,
        )

    loads = [
        pltpu.make_async_copy(src, dst, load_sem.at[i])
        for i, (src, dst) in enumerate(
            [
                (tokens_hbm, tok),
                (w_gate_hbm.at[0], w_gate),
                (w_up_hbm.at[0], w_up),
                (w_down_hbm.at[0], w_down),
            ]
        )
    ]
    for load in loads:
        load.start()

    barrier = pltpu.get_barrier_semaphore()

    @pl.loop(1, 8)
    def _(j):
        cd = (c + j % 2) % 2
        along_y = x * 8 + (y + j // 2) % 4 * 2 + cd
        pl.semaphore_signal(barrier, inc=1, device_id=(group, along_y), device_id_type=MESH)

        @pl.when(j > 1)
        def _():
            along_x = (x + j // 2) % 4 * 8 + y * 2 + cd
            pl.semaphore_signal(barrier, inc=1, device_id=(group, along_x), device_id_type=MESH)

    for to in (stride, groups - stride):
        pl.semaphore_signal(
            barrier, inc=1, device_id=((group + to) % groups, me), device_id_type=MESH
        )

    index = index_ref[...]
    experts = iota((EXPERTS, 256), 0)
    named = (experts == index[0:1, :]) | (experts == index[1:2, :])
    named_b = named.astype(F32).astype(BF16)
    earlier = (iota((256, 256), 0) < iota((256, 256), 1)).astype(F32).astype(BF16)
    place = jnp.dot(named_b, earlier, preferred_element_type=F32)
    spot[...] = jnp.where(named, place, -1.0)
    counts = jnp.dot(named_b, jnp.ones((256, 128), BF16), preferred_element_type=F32)
    count_out[...] = counts
    count_relay[x] = count_out[pl.ds(pl.multiple_of(x * 8, 8), 8), :]
    loads[0].wait()

    piece_id = iota((PIECE, 256), 0)

    def pack(q):
        slot_id = (piece_id + q * PIECE).astype(F32)

        @pl.loop(0, 4)
        def _(xd):
            lines = spot[pl.ds(pl.multiple_of(xd * 8, 8), 8), :]
            placer = jnp.concatenate(
                [(lines[j : j + 1, :] == slot_id).astype(F32) for j in range(8)], axis=0
            )
            packed = jnp.dot(placer.astype(BF16), tok[...], preferred_element_type=F32)
            send[q, xd] = packed.astype(BF16).reshape(8, PIECE, 2 * half)

    def start_first(q):
        @pl.loop(1, 4)
        def _(d):
            a1(q, d).start()
            b1(q, d).start()

        own(q, 0).start()
        own(q, 1).start()

    pack(0)
    pl.semaphore_wait(barrier, 15)

    @pl.loop(1, 4)
    def _(d):
        count_near(d).start()

    start_first(0)
    pack(1)
    several(count_relay.at[0:3], cnt_sem.at[1]).wait_recv()

    @pl.loop(1, 8)
    def _(j):
        count_far(j).start()

    count_in[c * 4 + y] = count_relay[...]
    start_first(1)

    for q in range(SPLIT):
        slot_id = (piece_id + q * PIECE).astype(F32)

        @pl.loop(0, 4)
        def _(xd):
            lines = spot[pl.ds(pl.multiple_of(xd * 8, 8), 8), :]
            weight = gate_ref[pl.ds(xd // 2, 1), :]
            spread = jnp.concatenate(
                [jnp.where(lines[j : j + 1, :] == slot_id, weight, 0.0) for j in range(8)], axis=0
            )
            rows = pl.ds(pl.multiple_of(xd * 8 * PIECE, 8 * PIECE), 8 * PIECE)
            scaled[q, rows, :] = spread.astype(BF16)

    several(count_in.at[0:7], cnt_sem.at[3]).wait_recv()

    def place_of(r):
        return r % 4 * 8 + r // 4 % 4 * 2 + r // 16

    arrived = count_in[...].reshape(8 * EXPERTS, 128).astype(BF16)
    row = iota((EXPERTS, 8 * EXPERTS), 0)
    col = iota((EXPERTS, 8 * EXPERTS), 1)
    here = col % 8 == y * 2 + c
    pick = (here & (col // 8 == row)).astype(F32).astype(BF16)
    before = (here & (place_of(col // 8) < place_of(row))).astype(F32).astype(BF16)
    count = jnp.dot(pick, arrived, preferred_element_type=F32)
    offset = jnp.dot(before, arrived, preferred_element_type=F32)
    limit = capacity_ref[0, 0].astype(F32)
    spare = jnp.maximum(limit - jnp.sum(count, axis=0, keepdims=True), 0.0)
    spare_out[...] = jnp.broadcast_to(spare, (8, 128))
    spare_copy(0).start()
    for q in range(SPLIT):
        several(relay_a.at[q, :, 0:3], near_recv.at[0, q]).wait_recv()
        several(relay_b.at[q, :, :, 0:3], near_recv.at[1, q]).wait_recv()
        own(q, 0).wait()
        own(q, 1).wait()

        @pl.loop(0, 2)
        def _(dc):
            @pl.loop(0, 4)
            def _(d):
                @pl.when(d + dc > 0)
                def _():
                    a2(q, d, dc).start()
                    b2(q, d, dc).start()

        own(q, 2).start()
        own(q, 3).start()
        if q == 0:
            spare_copy(0).wait_recv()
            spare_copy(1).start()

    spare_copy(1).wait_recv()
    room = limit + jnp.minimum(spare_in[0:1, :], float(BLOCK))
    kept = jnp.minimum(jnp.maximum(room - offset, 0.0), count).astype(BF16)
    for load in loads[1:]:
        load.wait()

    for q in range(SPLIT):
        own(q, 2).wait()
        own(q, 3).wait()

        @pl.loop(0, 2)
        def _(dc):
            core = (c + dc) % 2

            @pl.when(dc == 0)
            def _():
                several(relay_a.at[q, 0:3], far_recv.at[0, q, 0]).wait_recv()
                several(relay_a.at[q, 0:3], far_recv.at[1, q, 0]).wait_recv()

            @pl.when(dc == 1)
            def _():
                several(relay_a.at[q, 0:4], far_recv.at[0, q, 1]).wait_recv()
                several(relay_a.at[q, 0:4], far_recv.at[1, q, 1]).wait_recv()

            source = core * 16 + iota((ROWS, EXPERTS), 0) // PIECE
            pick = (source == iota((ROWS, EXPERTS), 1)).astype(F32).astype(BF16)
            most = jnp.dot(pick, kept, preferred_element_type=F32)[:, 0:1]
            keep = (iota((ROWS, 1), 0) % PIECE + q * PIECE).astype(F32) < most
            rows = recv[q, core].reshape(ROWS, 2 * half)
            for f in range(3):
                cols = pl.ds(f * 256, 256)
                gated = jnp.dot(rows, w_gate[:, cols], preferred_element_type=F32)
                upward = jnp.dot(rows, w_up[:, cols], preferred_element_type=F32)
                value = gated / (1.0 + jnp.exp(-gated)) * upward
                hidden[:, cols] = jnp.where(keep, value, 0.0).astype(BF16)
            h = hidden[...]
            for d in range(4):
                cols = pl.ds(d * 512, 512)
                result = jnp.dot(h, w_down[:, cols], preferred_element_type=F32)
                answer[q, core, :, :, :, cols] = result.astype(BF16).reshape(4, 4, PIECE, 512)

            @pl.loop(0, 4)
            def _(d):
                @pl.when(d + dc > 0)
                def _():
                    c1(q, d, dc).start()
                    d1(q, d, dc).start()

        own(q, 4).start()
        own(q, 5).start()

    for q in range(SPLIT):
        several(relay_a.at[q, 0:7], ret_recv.at[0, q]).wait_recv()
        several(relay_a.at[q, 0:7], ret_recv.at[1, q]).wait_recv()
        own(q, 4).wait()
        own(q, 5).wait()

        @pl.loop(1, 4)
        def _(d):
            c2(q, d).start()
            d2(q, d).start()

        own(q, 6).start()
        own(q, 7).start()

    for q in range(SPLIT):
        several(relay_a.at[q, :, 0:3], near_recv.at[2, q]).wait_recv()
        several(relay_a.at[q, :, 0:3], near_recv.at[3, q]).wait_recv()
        own(q, 6).wait()
        own(q, 7).wait()
        part = lax.dot_general(
            scaled[q],
            back[q].reshape(EXPERTS * PIECE, 2 * half),
            (((0,), (0,)), ((), ())),
            preferred_element_type=F32,
        )
        if q == 0:
            total[...] = part
        else:
            mixed_ref[...] = (total[...] + part).astype(BF16)

    several(count_relay.at[0:3], cnt_sem.at[0]).wait_send()
    several(count_in.at[0:7], cnt_sem.at[2]).wait_send()
    spare_copy(0).wait_send()
    spare_copy(1).wait_send()
    for way in range(4):
        several(relay_a.at[:, :, 0:3], near_send.at[way]).wait_send()
        several(relay_a.at[:, 0:7], far_send.at[way]).wait_send()


def on_device(tokens, chosen_expert_index, routing_gate_weight, w_gate, w_up, w_down, capacity):
    rows, width = tokens.shape
    units = w_gate.shape[2]
    half = width // 2
    hbm = pl.BlockSpec(memory_space=pl.ANY)
    vmem = pl.BlockSpec(memory_space=pltpu.VMEM)
    smem = pl.BlockSpec(memory_space=pltpu.SMEM)
    dma = pltpu.SemaphoreType.DMA
    wide = pltpu.VMEM((SPLIT, 4, 8, PIECE, width), BF16)
    by_source = pltpu.VMEM((SPLIT, 2, 4, 4, PIECE, width), BF16)
    relay_a = pltpu.VMEM((SPLIT, 8, 4, PIECE, half), BF16)
    relay_b = pltpu.VMEM((SPLIT, 4, 2, 4, PIECE, half), BF16)
    return pl.pallas_call(
        kernel,
        out_shape=jax.ShapeDtypeStruct((rows, width), BF16),
        in_specs=[hbm, vmem, vmem, hbm, hbm, hbm, smem],
        out_specs=vmem,
        scratch_shapes=[
            pltpu.VMEM((rows, width), BF16),
            pltpu.VMEM((width, units), BF16),
            pltpu.VMEM((width, units), BF16),
            pltpu.VMEM((units, width), BF16),
            wide,
            relay_a,
            relay_b,
            by_source,
            by_source,
            relay_a,
            relay_b,
            wide,
            pltpu.VMEM((EXPERTS, rows), F32),
            pltpu.VMEM((SPLIT, EXPERTS * PIECE, rows), BF16),
            pltpu.VMEM((ROWS, units), BF16),
            pltpu.VMEM((rows, width), F32),
            pltpu.VMEM((EXPERTS, 128), F32),
            pltpu.VMEM((4, 8, 128), F32),
            pltpu.VMEM((8, 4, 8, 128), F32),
            pltpu.VMEM((8, 128), F32),
            pltpu.VMEM((8, 128), F32),
            pltpu.VMEM((8, 128), F32),
            dma((4,)),
            dma((SPLIT, 8)),
            dma((4,)),
            dma((4,)),
            dma((4,)),
            dma((4, SPLIT)),
            dma((4,)),
            dma((2, SPLIT, 2)),
            dma((2, SPLIT)),
        ],
        compiler_params=pltpu.CompilerParams(
            collective_id=0, has_side_effects=True, vmem_limit_bytes=60 * 2**20
        ),
        cost_estimate=pl.CostEstimate(
            flops=6 * EXPERTS * SLOT * width * units,
            bytes_accessed=6 * width * units,
            transcendentals=0,
        ),
    )(
        tokens,
        chosen_expert_index[:, :8].T,
        routing_gate_weight[:, :8].T,
        w_gate,
        w_up,
        w_down,
        capacity,
    )


def solution(mesh):
    return jax.shard_map(
        on_device,
        mesh=mesh,
        in_specs=(
            P(("dp", "expert"), None),
            P(("dp", "expert"), None),
            P(("dp", "expert"), None),
            P("expert", None, None),
            P("expert", None, None),
            P("expert", None, None),
            P("dp", "expert"),
        ),
        out_specs=P(("dp", "expert"), None),
        check_vma=False,
    )
```

time: 112 us -> 108 us (0.964)
  Pallas kernels: 108 us -> 104 us
    pallas_call x1, Pallas kernels: 108 us -> 104 us  [on_device(): pl.pallas_call(kernel, out_shape=jax.ShapeDtypeStruct((rows, width), BF16...]
where the time goes in v4:
time: 108 us; the launch traced here: 107 us
  Pallas kernels  104 us (96%)
  local copies, waits for them, and re-layouts  2.3 us (2%)
    pallas_call x1, Pallas kernels, on_device(): pl.pallas_call(kernel, out_shape=jax.ShapeDtypeStruct((rows, width), BF16...  104 us
    unnamed x1, local copies, waits for them, and re-layouts  2.3 us

profile of v4, /device:TPU:1, one launch (start us, length us, event | category | flops | bytes accessed | tf_op | source)
XLA Modules:
  0.0 107.4 jit_solution(8124538059744567146)
XLA Ops:
  0.7 104.4 %shard_map.73 = bf16[256,2048]{1,0:T(8,128)(2,1)} custom-call(bf16[256,2048]{1,0:T(8,128)(2,1)} %tokens_hbm.1, s32[8,256]{1,0:T(8,128)} %bitcast.2, f32[8,256]{1,0:T(8,128)} %bitcast.3, bf16[1,2048,768]{2,1,0:T(8,128)(2,1)} %w_gate_hbm.1, bf16[1,2048,768]{2,1,0:T(8,128)(2,1)} %w_up_hbm.1, bf16[1,768,2048]{2,1,0:T(8,128)(2,1)} %w_down_hbm.1, ...), custom_call_target="tpu_custom_call" | custom-call | flops 9663676416 | bytes 9437184 | tf_op jit(solution)/shard_map/pallas_call | solution.py:382
  105.1 2.3 %copy.10 = bf16[256,2048]{1,0:T(8,128)(2,1)} copy(bf16[256,2048]{1,0:T(8,128)(2,1)} %shard_map.73) | data formatting | bytes 2097152

commit v5 on v4

--- a/solution.py
+++ b/solution.py
@@ -23,9 +23,9 @@
 def kernel(
     tokens_hbm, index_ref, gate_ref, w_gate_hbm, w_up_hbm, w_down_hbm, capacity_ref,
     mixed_ref,
-    tok, w_gate, w_up, w_down, send, relay_a, relay_b, recv, answer, home_a, home_b, back,
-    spot, scaled, hidden, total, count_out, count_relay, count_in, spare_out, spare_mid, spare_in,
-    load_sem, local_sem, cnt_sem, spare_sem, near_send, near_recv, far_send, far_recv, ret_recv,
+    tok, w_gate, w_up, w_down, ring_a, ring_b, relay_a, relay_b, recv, answer, home_a, home_b, back,
+    spot, spot_x, spot_y, scaled, hidden, total, count_relay, count_in, spare_out, spare_mid, spare_in,
+    load_sem, local_sem, spot_sem, cnt_sem, spare_sem, ring_send, ring_recv, near_send, near_recv, far_send, far_recv, ret_recv,
 ):
     me = lax.axis_index("expert")
     group = lax.axis_index("dp")
@@ -48,31 +48,39 @@
     def several(ref, sem):
         return remote(ref, ref, sem, sem, x, y, 1 - c)
 
-    def a1(q, dx):
-        xd = (x + dx) % 4
-        return remote(
-            send.at[q, xd, :, :, low], relay_a.at[q, :, x],
-            near_send.at[0], near_recv.at[0, q], xd, y, c,
-        )
-
-    def b1(q, dy):
-        yd = (y + dy) % 4
-        return remote(
-            send.at[q, :, pl.ds(yd * 2, 2), :, high], relay_b.at[q, :, :, y],
-            near_send.at[1], near_recv.at[1, q], x, yd, c,
-        )
-
-    def a2(q, d, dc):
+    first, second = pl.ds(0, tok.shape[0] // 2), pl.ds(tok.shape[0] // 2, tok.shape[0] // 2)
+
+    def ring(way, order, axis):
+        at, store, cols = [(x, ring_a, low), (y, ring_b, high)][axis]
+        step = [1, 3][way]
+        rows = [first, second] if way == 0 else [second, first]
+        to = (at + step) % 4
+        if order < 2:
+            src, dst = tok.at[rows[order], cols], store.at[at, rows[order]]
+        else:
+            behind = (at + 4 - step) % 4
+            src = dst = store.at[behind, rows[0]]
+        return remote(
+            src, dst, ring_send.at[axis], ring_recv.at[axis, way, order],
+            to if axis == 0 else x, y if axis == 0 else to, c,
+        )
+
+    def spot_copy(d, axis):
+        if axis == 0:
+            return remote(spot, spot_x.at[x], spot_sem.at[0], spot_sem.at[1], (x + d) % 4, y, c)
+        return remote(spot, spot_y.at[y], spot_sem.at[2], spot_sem.at[3], x, (y + d) % 4, c)
+
+    def a2(q, d, dc, xs=slice(None)):
         yd, cd = (y + d) % 4, (c + dc) % 2
         return remote(
-            relay_a.at[q, yd * 2 + cd], recv.at[q, c, y, :, :, low],
+            relay_a.at[q, yd * 2 + cd, xs], recv.at[q, c, y, xs, :, low],
             far_send.at[0], far_recv.at[0, q, dc], x, yd, cd,
         )
 
-    def b2(q, d, dc):
+    def b2(q, d, dc, ys=slice(None)):
         xd, cd = (x + d) % 4, (c + dc) % 2
         return remote(
-            relay_b.at[q, xd, cd], recv.at[q, c, :, x, :, high],
+            relay_b.at[q, xd, cd, ys], recv.at[q, c, ys, x, :, high],
             far_send.at[1], far_recv.at[1, q, dc], xd, y, cd,
         )
 
@@ -94,40 +102,31 @@
         xd = (x + dx) % 4
         return remote(
             home_a.at[q, :, xd], back.at[q, x, :, :, low],
-            near_send.at[2], near_recv.at[2, q], xd, y, c,
+            near_send.at[0], near_recv.at[0, q], xd, y, c,
         )
 
     def d2(q, dy):
         yd = (y + dy) % 4
         return remote(
             home_b.at[q, :, :, yd], back.at[q, :, pl.ds(y * 2, 2), :, high],
-            near_send.at[3], near_recv.at[3, q], x, yd, c,
+            near_send.at[1], near_recv.at[1, q], x, yd, c,
         )
 
     def own(q, hop):
         src, dst = [
-            (send.at[q, x, :, :, low], relay_a.at[q, :, x]),
-            (send.at[q, :, pl.ds(y * 2, 2), :, high], relay_b.at[q, :, :, y]),
             (relay_a.at[q, y * 2 + c], recv.at[q, c, y, :, :, low]),
             (relay_b.at[q, x, c], recv.at[q, c, :, x, :, high]),
             (answer.at[q, c, y, :, :, low], home_a.at[q, y * 2 + c]),
             (answer.at[q, c, :, x, :, high], home_b.at[q, x, c]),
             (home_a.at[q, :, x], back.at[q, x, :, :, low]),
             (home_b.at[q, :, :, y], back.at[q, :, pl.ds(y * 2, 2), :, high]),
-        ][hop]
-        return pltpu.make_async_copy(src, dst, local_sem.at[q, hop])
-
-    def count_near(dx):
-        xd = (x + dx) % 4
-        return remote(
-            count_out.at[pl.ds(pl.multiple_of(xd * 8, 8), 8), :], count_relay.at[x],
-            cnt_sem.at[0], cnt_sem.at[1], xd, y, c,
-        )
+        ][hop - 2]
+        return pltpu.make_async_copy(src, dst, local_sem.at[q, hop - 2])
 
     def count_far(j):
         return remote(
             count_relay, count_in.at[c * 4 + y],
-            cnt_sem.at[2], cnt_sem.at[3], x, (y + j // 2) % 4, (c + j % 2) % 2,
+            cnt_sem.at[0], cnt_sem.at[1], x, (y + j // 2) % 4, (c + j % 2) % 2,
         )
 
     def spare_copy(hop):
@@ -179,52 +178,82 @@
     named_b = named.astype(F32).astype(BF16)
     earlier = (iota((256, 256), 0) < iota((256, 256), 1)).astype(F32).astype(BF16)
     place = jnp.dot(named_b, earlier, preferred_element_type=F32)
-    spot[...] = jnp.where(named, place, -1.0)
-    counts = jnp.dot(named_b, jnp.ones((256, 128), BF16), preferred_element_type=F32)
-    count_out[...] = counts
-    count_relay[x] = count_out[pl.ds(pl.multiple_of(x * 8, 8), 8), :]
+    placed = jnp.where(named, place, -1.0)
+    spot[...] = placed
+    spot_x[x] = placed
+    spot_y[y] = placed
     loads[0].wait()
 
     piece_id = iota((PIECE, 256), 0)
-
-    def pack(q):
-        slot_id = (piece_id + q * PIECE).astype(F32)
-
-        @pl.loop(0, 4)
-        def _(xd):
-            lines = spot[pl.ds(pl.multiple_of(xd * 8, 8), 8), :]
-            placer = jnp.concatenate(
-                [(lines[j : j + 1, :] == slot_id).astype(F32) for j in range(8)], axis=0
-            )
-            packed = jnp.dot(placer.astype(BF16), tok[...], preferred_element_type=F32)
-            send[q, xd] = packed.astype(BF16).reshape(8, PIECE, 2 * half)
-
-    def start_first(q):
-        @pl.loop(1, 4)
-        def _(d):
-            a1(q, d).start()
-            b1(q, d).start()
-
-        own(q, 0).start()
-        own(q, 1).start()
-
-    pack(0)
     pl.semaphore_wait(barrier, 15)
 
     @pl.loop(1, 4)
     def _(d):
-        count_near(d).start()
-
-    start_first(0)
-    pack(1)
-    several(count_relay.at[0:3], cnt_sem.at[1]).wait_recv()
+        spot_copy(d, 0).start()
+        spot_copy(d, 1).start()
+
+    for order in range(2):
+        for axis in range(2):
+            for way in range(2):
+                ring(way, order, axis).start()
+
+    def pack(o):
+        xs, ys = (x + o) % 4, (y + o) % 4
+        rows_a = tok[:, low] if o == 0 else ring_a[xs]
+        rows_b = tok[:, high] if o == 0 else ring_b[ys]
+        lines_a = spot_x[xs, pl.ds(pl.multiple_of(x * 8, 8), 8), :]
+        lines_a = [lines_a[j : j + 1, :] for j in range(8)]
+        lines_b = [spot_y[ys, pl.ds(j // 2 * 8 + y * 2 + j % 2, 1), :] for j in range(8)]
+        for lines, rows, side in ((lines_a, rows_a, 0), (lines_b, rows_b, 1)):
+            placer = jnp.concatenate(
+                [
+                    (line == (piece_id + q * PIECE).astype(F32)).astype(F32)
+                    for q in range(SPLIT)
+                    for line in lines
+                ],
+                axis=0,
+            )
+            packed = jnp.dot(placer.astype(BF16), rows, preferred_element_type=F32).astype(BF16)
+            for q in range(SPLIT):
+                part = packed[q * 8 * PIECE : (q + 1) * 8 * PIECE]
+                if side == 0:
+                    relay_a[q, :, xs] = part.reshape(8, PIECE, half)
+                else:
+                    relay_b[q, :, :, ys] = part.reshape(4, 2, PIECE, half)
+
+    def start_second(q, o):
+        @pl.loop(0, 2)
+        def _(dc):
+            @pl.loop(0, 4)
+            def _(d):
+                @pl.when(d + dc > 0)
+                def _():
+                    if o is None:
+                        a2(q, d, dc).start()
+                        b2(q, d, dc).start()
+                    else:
+                        a2(q, d, dc, (x + o) % 4).start()
+                        b2(q, d, dc, (y + o) % 4).start()
+
+    pack(0)
+    several(spot_x.at[0:3], spot_sem.at[1]).wait_recv()
+    several(spot_y.at[0:3], spot_sem.at[3]).wait_recv()
+    for xs in range(4):
+        lines = spot_x[xs, pl.ds(pl.multiple_of(x * 8, 8), 8), :]
+        number = jnp.sum((lines >= 0.0).astype(F32), axis=1, keepdims=True)
+        count_relay[xs] = jnp.broadcast_to(number, (8, 128))
 
     @pl.loop(1, 8)
     def _(j):
         count_far(j).start()
 
     count_in[c * 4 + y] = count_relay[...]
-    start_first(1)
+    for axis in range(2):
+        for way in range(2):
+            ring(way, 0, axis).wait_recv()
+            ring(way, 2, axis).start()
+
+    start_second(0, 0)
 
     for q in range(SPLIT):
         slot_id = (piece_id + q * PIECE).astype(F32)
@@ -239,7 +268,7 @@
             rows = pl.ds(pl.multiple_of(xd * 8 * PIECE, 8 * PIECE), 8 * PIECE)
             scaled[q, rows, :] = spread.astype(BF16)
 
-    several(count_in.at[0:7], cnt_sem.at[3]).wait_recv()
+    several(count_in.at[0:7], cnt_sem.at[1]).wait_recv()
 
     def place_of(r):
         return r % 4 * 8 + r // 4 % 4 * 2 + r // 16
@@ -256,26 +285,25 @@
     spare = jnp.maximum(limit - jnp.sum(count, axis=0, keepdims=True), 0.0)
     spare_out[...] = jnp.broadcast_to(spare, (8, 128))
     spare_copy(0).start()
+    for axis in range(2):
+        ring(0, 1, axis).wait_recv()
+    pack(3)
+    start_second(0, 3)
+    for axis in range(2):
+        ring(1, 1, axis).wait_recv()
+    pack(1)
+    start_second(0, 1)
+    spare_copy(0).wait_recv()
+    spare_copy(1).start()
+    for axis in range(2):
+        for way in range(2):
+            ring(way, 2, axis).wait_recv()
+    pack(2)
+    start_second(0, 2)
+    start_second(1, None)
     for q in range(SPLIT):
-        several(relay_a.at[q, :, 0:3], near_recv.at[0, q]).wait_recv()
-        several(relay_b.at[q, :, :, 0:3], near_recv.at[1, q]).wait_recv()
-        own(q, 0).wait()
-        own(q, 1).wait()
-
-        @pl.loop(0, 2)
-        def _(dc):
-            @pl.loop(0, 4)
-            def _(d):
-                @pl.when(d + dc > 0)
-                def _():
-                    a2(q, d, dc).start()
-                    b2(q, d, dc).start()
-
         own(q, 2).start()
         own(q, 3).start()
-        if q == 0:
-            spare_copy(0).wait_recv()
-            spare_copy(1).start()
 
     spare_copy(1).wait_recv()
     room = limit + jnp.minimum(spare_in[0:1, :], float(BLOCK))
@@ -343,8 +371,8 @@
         own(q, 7).start()
 
     for q in range(SPLIT):
-        several(relay_a.at[q, :, 0:3], near_recv.at[2, q]).wait_recv()
-        several(relay_a.at[q, :, 0:3], near_recv.at[3, q]).wait_recv()
+        several(relay_a.at[q, :, 0:3], near_recv.at[0, q]).wait_recv()
+        several(relay_a.at[q, :, 0:3], near_recv.at[1, q]).wait_recv()
         own(q, 6).wait()
         own(q, 7).wait()
         part = lax.dot_general(
@@ -358,12 +386,15 @@
         else:
             mixed_ref[...] = (total[...] + part).astype(BF16)
 
-    several(count_relay.at[0:3], cnt_sem.at[0]).wait_send()
-    several(count_in.at[0:7], cnt_sem.at[2]).wait_send()
+    several(spot_x.at[0:3], spot_sem.at[0]).wait_send()
+    several(spot_x.at[0:3], spot_sem.at[2]).wait_send()
+    several(count_in.at[0:7], cnt_sem.at[0]).wait_send()
     spare_copy(0).wait_send()
     spare_copy(1).wait_send()
+    for way in range(2):
+        several(ring_a.at[0:3], ring_send.at[way]).wait_send()
+        several(relay_a.at[:, :, 0:3], near_send.at[way]).wait_send()
     for way in range(4):
-        several(relay_a.at[:, :, 0:3], near_send.at[way]).wait_send()
         several(relay_a.at[:, 0:7], far_send.at[way]).wait_send()
 
 
@@ -389,7 +420,8 @@
             pltpu.VMEM((width, units), BF16),
             pltpu.VMEM((width, units), BF16),
             pltpu.VMEM((units, width), BF16),
-            wide,
+            pltpu.VMEM((4, rows, half), BF16),
+            pltpu.VMEM((4, rows, half), BF16),
             relay_a,
             relay_b,
             by_source,
@@ -398,21 +430,25 @@
             relay_b,
             wide,
             pltpu.VMEM((EXPERTS, rows), F32),
+            pltpu.VMEM((4, EXPERTS, rows), F32),
+            pltpu.VMEM((4, EXPERTS, rows), F32),
             pltpu.VMEM((SPLIT, EXPERTS * PIECE, rows), BF16),
             pltpu.VMEM((ROWS, units), BF16),
             pltpu.VMEM((rows, width), F32),
-            pltpu.VMEM((EXPERTS, 128), F32),
             pltpu.VMEM((4, 8, 128), F32),
             pltpu.VMEM((8, 4, 8, 128), F32),
             pltpu.VMEM((8, 128), F32),
             pltpu.VMEM((8, 128), F32),
             pltpu.VMEM((8, 128), F32),
             dma((4,)),
-            dma((SPLIT, 8)),
+            dma((SPLIT, 6)),
             dma((4,)),
+            dma((2,)),
             dma((4,)),
-            dma((4,)),
-            dma((4, SPLIT)),
+            dma((2,)),
+            dma((2, 2, 3)),
+            dma((2,)),
+            dma((2, SPLIT)),
             dma((4,)),
             dma((2, SPLIT, 2)),
             dma((2, SPLIT)),

time: 108 us -> 103 us (0.954)
  Pallas kernels: 104 us -> 100 us
    pallas_call x1, Pallas kernels: 104 us -> 100 us  [on_device(): pl.pallas_call(kernel, out_shape=jax.ShapeDtypeStruct((rows, width), BF16...]
where the time goes in v5:
time: 103 us
  Pallas kernels  100 us (97%)
  local copies, waits for them, and re-layouts  2.3 us (2%)
    pallas_call x1, Pallas kernels, on_device(): pl.pallas_call(kernel, out_shape=jax.ShapeDtypeStruct((rows, width), BF16...  100 us
    unnamed x1, local copies, waits for them, and re-layouts  2.3 us

profile of v5, /device:TPU:1, one launch (start us, length us, event | category | flops | bytes accessed | tf_op | source)
XLA Modules:
  0.0 103.1 jit_solution(3831523515652455395)
XLA Ops:
  0.7 100.1 %shard_map.73 = bf16[256,2048]{1,0:T(8,128)(2,1)} custom-call(bf16[256,2048]{1,0:T(8,128)(2,1)} %tokens_hbm.1, s32[8,256]{1,0:T(8,128)} %bitcast.2, f32[8,256]{1,0:T(8,128)} %bitcast.3, bf16[1,2048,768]{2,1,0:T(8,128)(2,1)} %w_gate_hbm.1, bf16[1,2048,768]{2,1,0:T(8,128)(2,1)} %w_up_hbm.1, bf16[1,768,2048]{2,1,0:T(8,128)(2,1)} %w_down_hbm.1, ...), custom_call_target="tpu_custom_call" | custom-call | flops 9663676416 | bytes 9437184 | tf_op jit(solution)/shard_map/pallas_call | solution.py:413
  100.8 2.3 %copy.10 = bf16[256,2048]{1,0:T(8,128)(2,1)} copy(bf16[256,2048]{1,0:T(8,128)(2,1)} %shard_map.73) | data formatting | bytes 2097152

commit v6 on v5

--- a/solution.py
+++ b/solution.py
@@ -23,9 +23,10 @@
 def kernel(
     tokens_hbm, index_ref, gate_ref, w_gate_hbm, w_up_hbm, w_down_hbm, capacity_ref,
     mixed_ref,
-    tok, w_gate, w_up, w_down, ring_a, ring_b, relay_a, relay_b, recv, answer, home_a, home_b, back,
-    spot, spot_x, spot_y, scaled, hidden, total, count_relay, count_in, spare_out, spare_mid, spare_in,
-    load_sem, local_sem, spot_sem, cnt_sem, spare_sem, ring_send, ring_recv, near_send, near_recv, far_send, far_recv, ret_recv,
+    tok, w_gate, w_up, w_down, ring_a, ring_b, relay_a, relay_b, recv, answer, home_a, home_b,
+    sum_a, sum_b, far_a, far_b, near_a, near_b,
+    spot, spot_x, spot_y, spot_a, spot_b, scaled_a, scaled_b, hidden, total, count_relay, count_in, spare_out, spare_mid, spare_in,
+    load_sem, local_sem, spot_sem, cnt_sem, spare_sem, ring_send, ring_recv, sum_send, sum_recv, far_send, far_recv, ret_recv,
 ):
     me = lax.axis_index("expert")
     group = lax.axis_index("dp")
@@ -84,32 +85,35 @@
             far_send.at[1], far_recv.at[1, q, dc], xd, y, cd,
         )
 
-    def c1(q, d, dc):
+    def c1(q, d, dc, o=None):
         yd, cd = (y + d) % 4, (c + dc) % 2
-        return remote(
-            answer.at[q, cd, yd, :, :, low], home_a.at[q, y * 2 + c],
-            far_send.at[2], ret_recv.at[0, q], x, yd, cd,
-        )
-
-    def d1(q, d, dc):
+        xs = slice(None) if o is None else (x + o) % 4
+        return remote(
+            answer.at[q, cd, yd, xs, :, low], home_a.at[q, y * 2 + c, xs],
+            far_send.at[2], ret_recv.at[0, 2 if o == 2 else q], x, yd, cd,
+        )
+
+    def d1(q, d, dc, o=None):
         xd, cd = (x + d) % 4, (c + dc) % 2
-        return remote(
-            answer.at[q, cd, :, xd, :, high], home_b.at[q, x, c],
-            far_send.at[3], ret_recv.at[1, q], xd, y, cd,
-        )
-
-    def c2(q, dx):
-        xd = (x + dx) % 4
-        return remote(
-            home_a.at[q, :, xd], back.at[q, x, :, :, low],
-            near_send.at[0], near_recv.at[0, q], xd, y, c,
-        )
-
-    def d2(q, dy):
-        yd = (y + dy) % 4
-        return remote(
-            home_b.at[q, :, :, yd], back.at[q, :, pl.ds(y * 2, 2), :, high],
-            near_send.at[1], near_recv.at[1, q], x, yd, c,
+        ys = slice(None) if o is None else (y + o) % 4
+        return remote(
+            answer.at[q, cd, ys, xd, :, high], home_b.at[q, x, c, ys],
+            far_send.at[3], ret_recv.at[1, 2 if o == 2 else q], xd, y, cd,
+        )
+
+    def sums(way, order, axis):
+        at = [x, y][axis]
+        store, far, near = [(sum_a, far_a, near_a), (sum_b, far_b, near_b)][axis]
+        rows = [first, second] if way == 0 else [second, first]
+        to = (at + [1, 3][way]) % 4
+        if order == 0:
+            src, dst = store.at[0, rows[0]], far.at[way]
+        else:
+            half_of = rows[2 - order]
+            src, dst = store.at[1 + way, half_of], near.at[way, half_of]
+        return remote(
+            src, dst, sum_send.at[axis], sum_recv.at[axis, way, order],
+            to if axis == 0 else x, y if axis == 0 else to, c,
         )
 
     def own(q, hop):
@@ -118,8 +122,6 @@
             (relay_b.at[q, x, c], recv.at[q, c, :, x, :, high]),
             (answer.at[q, c, y, :, :, low], home_a.at[q, y * 2 + c]),
             (answer.at[q, c, :, x, :, high], home_b.at[q, x, c]),
-            (home_a.at[q, :, x], back.at[q, x, :, :, low]),
-            (home_b.at[q, :, :, y], back.at[q, :, pl.ds(y * 2, 2), :, high]),
         ][hop - 2]
         return pltpu.make_async_copy(src, dst, local_sem.at[q, hop - 2])
 
@@ -173,15 +175,12 @@
         )
 
     index = index_ref[...]
-    experts = iota((EXPERTS, 256), 0)
-    named = (experts == index[0:1, :]) | (experts == index[1:2, :])
-    named_b = named.astype(F32).astype(BF16)
+    spot[pl.ds(0, 2), :] = index[0:2, :].astype(F32)
+    spot[pl.ds(2, 2), :] = gate_ref[0:2, :]
+    spot[pl.ds(4, 4), :] = jnp.zeros((4, 256), F32)
+    spot_x[x] = spot[...]
+    spot_y[y] = spot[...]
     earlier = (iota((256, 256), 0) < iota((256, 256), 1)).astype(F32).astype(BF16)
-    place = jnp.dot(named_b, earlier, preferred_element_type=F32)
-    placed = jnp.where(named, place, -1.0)
-    spot[...] = placed
-    spot_x[x] = placed
-    spot_y[y] = placed
     loads[0].wait()
 
     piece_id = iota((PIECE, 256), 0)
@@ -201,9 +200,9 @@
         xs, ys = (x + o) % 4, (y + o) % 4
         rows_a = tok[:, low] if o == 0 else ring_a[xs]
         rows_b = tok[:, high] if o == 0 else ring_b[ys]
-        lines_a = spot_x[xs, pl.ds(pl.multiple_of(x * 8, 8), 8), :]
+        lines_a, lines_b = spot_a[xs], spot_b[ys]
         lines_a = [lines_a[j : j + 1, :] for j in range(8)]
-        lines_b = [spot_y[ys, pl.ds(j // 2 * 8 + y * 2 + j % 2, 1), :] for j in range(8)]
+        lines_b = [lines_b[j : j + 1, :] for j in range(8)]
         for lines, rows, side in ((lines_a, rows_a, 0), (lines_b, rows_b, 1)):
             placer = jnp.concatenate(
                 [
@@ -235,12 +234,22 @@
                         a2(q, d, dc, (x + o) % 4).start()
                         b2(q, d, dc, (y + o) % 4).start()
 
-    pack(0)
     several(spot_x.at[0:3], spot_sem.at[1]).wait_recv()
     several(spot_y.at[0:3], spot_sem.at[3]).wait_recv()
+    j = iota((8, 256), 0)
+    for store, meta, ids in ((spot_a, spot_x, x * 8 + j), (spot_b, spot_y, j // 2 * 8 + y * 2 + j % 2)):
+        ids = ids.astype(F32)
+        named = jnp.concatenate(
+            [
+                ((meta[at, 0:1, :] == ids) | (meta[at, 1:2, :] == ids)).astype(F32)
+                for at in range(4)
+            ],
+            axis=0,
+        )
+        place = jnp.dot(named.astype(BF16), earlier, preferred_element_type=F32)
+        store[...] = jnp.where(named > 0.0, place, -1.0).reshape(4, 8, 256)
     for xs in range(4):
-        lines = spot_x[xs, pl.ds(pl.multiple_of(x * 8, 8), 8), :]
-        number = jnp.sum((lines >= 0.0).astype(F32), axis=1, keepdims=True)
+        number = jnp.sum((spot_a[xs] >= 0.0).astype(F32), axis=1, keepdims=True)
         count_relay[xs] = jnp.broadcast_to(number, (8, 128))
 
     @pl.loop(1, 8)
@@ -248,6 +257,7 @@
         count_far(j).start()
 
     count_in[c * 4 + y] = count_relay[...]
+    pack(0)
     for axis in range(2):
         for way in range(2):
             ring(way, 0, axis).wait_recv()
@@ -255,18 +265,20 @@
 
     start_second(0, 0)
 
-    for q in range(SPLIT):
-        slot_id = (piece_id + q * PIECE).astype(F32)
-
-        @pl.loop(0, 4)
-        def _(xd):
-            lines = spot[pl.ds(pl.multiple_of(xd * 8, 8), 8), :]
-            weight = gate_ref[pl.ds(xd // 2, 1), :]
-            spread = jnp.concatenate(
-                [jnp.where(lines[j : j + 1, :] == slot_id, weight, 0.0) for j in range(8)], axis=0
-            )
-            rows = pl.ds(pl.multiple_of(xd * 8 * PIECE, 8 * PIECE), 8 * PIECE)
-            scaled[q, rows, :] = spread.astype(BF16)
+    @pl.loop(0, 4)
+    def _(at):
+        lines_a, lines_b = spot_a[at], spot_b[at]
+        weight_a = spot_x[at, pl.ds(2 + x // 2, 1), :]
+        for j in range(8):
+            line_b = lines_b[j : j + 1, :]
+            weight_b = spot_y[at, pl.ds(2 + j // 4, 1), :]
+            for q in range(SPLIT):
+                slot_id = (piece_id + q * PIECE).astype(F32)
+                rows = pl.ds(j * PIECE, PIECE)
+                spread = jnp.where(lines_a[j : j + 1, :] == slot_id, weight_a, 0.0)
+                scaled_a[at, q, rows, :] = spread.astype(BF16)
+                spread = jnp.where(line_b == slot_id, weight_b, 0.0)
+                scaled_b[at, q, rows, :] = spread.astype(BF16)
 
     several(count_in.at[0:7], cnt_sem.at[1]).wait_recv()
 
@@ -346,45 +358,69 @@
                 result = jnp.dot(h, w_down[:, cols], preferred_element_type=F32)
                 answer[q, core, :, :, :, cols] = result.astype(BF16).reshape(4, 4, PIECE, 512)
 
-            @pl.loop(0, 4)
-            def _(d):
-                @pl.when(d + dc > 0)
-                def _():
-                    c1(q, d, dc).start()
-                    d1(q, d, dc).start()
+            for o in (None,) if q == 0 else (2, 1, 3, 0):
+
+                @pl.loop(0, 4)
+                def _(d):
+                    @pl.when(d + dc > 0)
+                    def _():
+                        c1(q, d, dc, o).start()
+                        d1(q, d, dc, o).start()
 
         own(q, 4).start()
         own(q, 5).start()
 
     for q in range(SPLIT):
-        several(relay_a.at[q, 0:7], ret_recv.at[0, q]).wait_recv()
-        several(relay_a.at[q, 0:7], ret_recv.at[1, q]).wait_recv()
         own(q, 4).wait()
         own(q, 5).wait()
-
-        @pl.loop(1, 4)
-        def _(d):
-            c2(q, d).start()
-            d2(q, d).start()
-
-        own(q, 6).start()
-        own(q, 7).start()
-
-    for q in range(SPLIT):
-        several(relay_a.at[q, :, 0:3], near_recv.at[0, q]).wait_recv()
-        several(relay_a.at[q, :, 0:3], near_recv.at[1, q]).wait_recv()
-        own(q, 6).wait()
-        own(q, 7).wait()
-        part = lax.dot_general(
-            scaled[q],
-            back[q].reshape(EXPERTS * PIECE, 2 * half),
-            (((0,), (0,)), ((), ())),
-            preferred_element_type=F32,
-        )
-        if q == 0:
-            total[...] = part
-        else:
-            mixed_ref[...] = (total[...] + part).astype(BF16)
+    for axis in range(2):
+        several(relay_a.at[0, 0:7], ret_recv.at[axis, 0]).wait_recv()
+        several(relay_a.at[0, 0:7, 0], ret_recv.at[axis, 2]).wait_recv()
+
+    def sum_for(o, axis):
+        at = ([x, y][axis] + o) % 4
+        result = None
+        for q in range(SPLIT):
+            rows = home_a[q, :, at] if axis == 0 else home_b[q, :, :, at]
+            share = lax.dot_general(
+                (scaled_a if axis == 0 else scaled_b)[at, q],
+                rows.reshape(8 * PIECE, half),
+                (((0,), (0,)), ((), ())),
+                preferred_element_type=F32,
+            )
+            result = share if result is None else result + share
+        return result
+
+    for axis in range(2):
+        store = [sum_a, sum_b][axis]
+        store[0] = sum_for(2, axis).astype(BF16)
+        for way in range(2):
+            sums(way, 0, axis).start()
+    for axis in range(2):
+        several(relay_a.at[0, 0:7, 0:3], ret_recv.at[axis, 1]).wait_recv()
+    for way in range(2):
+        for axis in range(2):
+            store = [sum_a, sum_b][axis]
+            store[1 + way] = sum_for([1, 3][way], axis).astype(BF16)
+            sums(way, 1, axis).start()
+    for axis in range(2):
+        total[:, [low, high][axis]] = sum_for(0, axis)
+    for way in range(2):
+        for axis in range(2):
+            store, far = [(sum_a, far_a), (sum_b, far_b)][axis]
+            rows = [first, second][way]
+            sums(way, 0, axis).wait_recv()
+            merged = store[1 + way, rows, :].astype(F32) + far[way].astype(F32)
+            store[1 + way, rows, :] = merged.astype(BF16)
+            sums(way, 2, axis).start()
+    for order in (1, 2):
+        for axis in range(2):
+            near, cols = [(near_a, low), (near_b, high)][axis]
+            for way in range(2):
+                sums(way, order, axis).wait_recv()
+                rows = [first, second][way if order == 2 else 1 - way]
+                total[rows, cols] += near[way, rows, :].astype(F32)
+    mixed_ref[...] = total[...].astype(BF16)
 
     several(spot_x.at[0:3], spot_sem.at[0]).wait_send()
     several(spot_x.at[0:3], spot_sem.at[2]).wait_send()
@@ -393,7 +429,7 @@
     spare_copy(1).wait_send()
     for way in range(2):
         several(ring_a.at[0:3], ring_send.at[way]).wait_send()
-        several(relay_a.at[:, :, 0:3], near_send.at[way]).wait_send()
+        several(ring_a.at[0:3], sum_send.at[way]).wait_send()
     for way in range(4):
         several(relay_a.at[:, 0:7], far_send.at[way]).wait_send()
 
@@ -406,7 +442,7 @@
     vmem = pl.BlockSpec(memory_space=pltpu.VMEM)
     smem = pl.BlockSpec(memory_space=pltpu.SMEM)
     dma = pltpu.SemaphoreType.DMA
-    wide = pltpu.VMEM((SPLIT, 4, 8, PIECE, width), BF16)
+    per_token = pltpu.VMEM((4, SPLIT, 8 * PIECE, rows), BF16)
     by_source = pltpu.VMEM((SPLIT, 2, 4, 4, PIECE, width), BF16)
     relay_a = pltpu.VMEM((SPLIT, 8, 4, PIECE, half), BF16)
     relay_b = pltpu.VMEM((SPLIT, 4, 2, 4, PIECE, half), BF16)
@@ -428,11 +464,19 @@
             by_source,
             relay_a,
             relay_b,
-            wide,
-            pltpu.VMEM((EXPERTS, rows), F32),
-            pltpu.VMEM((4, EXPERTS, rows), F32),
-            pltpu.VMEM((4, EXPERTS, rows), F32),
-            pltpu.VMEM((SPLIT, EXPERTS * PIECE, rows), BF16),
+            pltpu.VMEM((3, rows, half), BF16),
+            pltpu.VMEM((3, rows, half), BF16),
+            pltpu.VMEM((2, rows // 2, half), BF16),
+            pltpu.VMEM((2, rows // 2, half), BF16),
+            pltpu.VMEM((2, rows, half), BF16),
+            pltpu.VMEM((2, rows, half), BF16),
+            pltpu.VMEM((8, rows), F32),
+            pltpu.VMEM((4, 8, rows), F32),
+            pltpu.VMEM((4, 8, rows), F32),
+            pltpu.VMEM((4, 8, rows), F32),
+            pltpu.VMEM((4, 8, rows), F32),
+            per_token,
+            per_token,
             pltpu.VMEM((ROWS, units), BF16),
             pltpu.VMEM((rows, width), F32),
             pltpu.VMEM((4, 8, 128), F32),
@@ -441,17 +485,17 @@
             pltpu.VMEM((8, 128), F32),
             pltpu.VMEM((8, 128), F32),
             dma((4,)),
-            dma((SPLIT, 6)),
+            dma((SPLIT, 4)),
             dma((4,)),
             dma((2,)),
             dma((4,)),
             dma((2,)),
             dma((2, 2, 3)),
             dma((2,)),
-            dma((2, SPLIT)),
+            dma((2, 2, 3)),
             dma((4,)),
             dma((2, SPLIT, 2)),
-            dma((2, SPLIT)),
+            dma((2, SPLIT + 1)),
         ],
         compiler_params=pltpu.CompilerParams(
             collective_id=0, has_side_effects=True, vmem_limit_bytes=60 * 2**20

time: 103 us -> 96.8 us (0.940)
  Pallas kernels: 100 us -> 93.6 us
    pallas_call x1, Pallas kernels: 100 us -> 93.6 us  [on_device(): pl.pallas_call(kernel, out_shape=jax.ShapeDtypeStruct((rows, width), BF16...]
where the time goes in v6:
time: 96.8 us; the launch traced here: 96.6 us
  Pallas kernels  93.6 us (97%)
  local copies, waits for them, and re-layouts  2.3 us (2%)
    pallas_call x1, Pallas kernels, on_device(): pl.pallas_call(kernel, out_shape=jax.ShapeDtypeStruct((rows, width), BF16...  93.6 us
    unnamed x1, local copies, waits for them, and re-layouts  2.3 us

profile of v6, /device:TPU:1, one launch (start us, length us, event | category | flops | bytes accessed | tf_op | source)
XLA Modules:
  0.0 96.6 jit_solution(6934546748810315997)
XLA Ops:
  0.7 93.6 %shard_map.73 = bf16[256,2048]{1,0:T(8,128)(2,1)} custom-call(bf16[256,2048]{1,0:T(8,128)(2,1)} %tokens_hbm.1, s32[8,256]{1,0:T(8,128)} %bitcast.2, f32[8,256]{1,0:T(8,128)} %bitcast.3, bf16[1,2048,768]{2,1,0:T(8,128)(2,1)} %w_gate_hbm.1, bf16[1,2048,768]{2,1,0:T(8,128)(2,1)} %w_up_hbm.1, bf16[1,768,2048]{2,1,0:T(8,128)(2,1)} %w_down_hbm.1, ...), custom_call_target="tpu_custom_call" | custom-call | flops 9663676416 | bytes 9437184 | tf_op jit(solution)/shard_map/pallas_call | solution.py:449
  94.3 2.3 %copy.10 = bf16[256,2048]{1,0:T(8,128)(2,1)} copy(bf16[256,2048]{1,0:T(8,128)(2,1)} %shard_map.73) | data formatting | bytes 2097152

commit v7 on v6

--- a/solution.py
+++ b/solution.py
@@ -90,7 +90,7 @@
         xs = slice(None) if o is None else (x + o) % 4
         return remote(
             answer.at[q, cd, yd, xs, :, low], home_a.at[q, y * 2 + c, xs],
-            far_send.at[2], ret_recv.at[0, 2 if o == 2 else q], x, yd, cd,
+            far_send.at[2], ret_recv.at[0, q if o is None else 2 if o == 2 else 3 if o == 0 else 1], x, yd, cd,
         )
 
     def d1(q, d, dc, o=None):
@@ -98,7 +98,7 @@
         ys = slice(None) if o is None else (y + o) % 4
         return remote(
             answer.at[q, cd, ys, xd, :, high], home_b.at[q, x, c, ys],
-            far_send.at[3], ret_recv.at[1, 2 if o == 2 else q], xd, y, cd,
+            far_send.at[3], ret_recv.at[1, q if o is None else 2 if o == 2 else 3 if o == 0 else 1], xd, y, cd,
         )
 
     def sums(way, order, axis):
@@ -248,9 +248,12 @@
         )
         place = jnp.dot(named.astype(BF16), earlier, preferred_element_type=F32)
         store[...] = jnp.where(named > 0.0, place, -1.0).reshape(4, 8, 256)
+    lane = iota((8, 128), 1)
+    numbers = jnp.zeros((8, 128), F32)
     for xs in range(4):
         number = jnp.sum((spot_a[xs] >= 0.0).astype(F32), axis=1, keepdims=True)
-        count_relay[xs] = jnp.broadcast_to(number, (8, 128))
+        numbers = jnp.where(lane == xs, number, numbers)
+    count_relay[...] = numbers
 
     @pl.loop(1, 8)
     def _(j):
@@ -285,14 +288,16 @@
     def place_of(r):
         return r % 4 * 8 + r // 4 % 4 * 2 + r // 16
 
-    arrived = count_in[...].reshape(8 * EXPERTS, 128).astype(BF16)
-    row = iota((EXPERTS, 8 * EXPERTS), 0)
-    col = iota((EXPERTS, 8 * EXPERTS), 1)
-    here = col % 8 == y * 2 + c
-    pick = (here & (col // 8 == row)).astype(F32).astype(BF16)
-    before = (here & (place_of(col // 8) < place_of(row))).astype(F32).astype(BF16)
-    count = jnp.dot(pick, arrived, preferred_element_type=F32)
-    offset = jnp.dot(before, arrived, preferred_element_type=F32)
+    arrived = count_in[...].reshape(2 * EXPERTS, 128).astype(BF16)
+    row, col = iota((EXPERTS, 2 * EXPERTS), 0), iota((EXPERTS, 2 * EXPERTS), 1)
+    pick = (col == row // 4 * 8 + y * 2 + c).astype(F32).astype(BF16)
+    by_lane = jnp.dot(pick, arrived, preferred_element_type=F32)
+    chosen = iota((EXPERTS, 128), 1) == iota((EXPERTS, 128), 0) % 4
+    count = jnp.sum(jnp.where(chosen, by_lane, 0.0), axis=1, keepdims=True)
+    count = jnp.broadcast_to(count, (EXPERTS, 128))
+    row, col = iota((EXPERTS, EXPERTS), 0), iota((EXPERTS, EXPERTS), 1)
+    before = (place_of(col) < place_of(row)).astype(F32).astype(BF16)
+    offset = jnp.dot(before, count.astype(BF16), preferred_element_type=F32)
     limit = capacity_ref[0, 0].astype(F32)
     spare = jnp.maximum(limit - jnp.sum(count, axis=0, keepdims=True), 0.0)
     spare_out[...] = jnp.broadcast_to(spare, (8, 128))
@@ -358,7 +363,7 @@
                 result = jnp.dot(h, w_down[:, cols], preferred_element_type=F32)
                 answer[q, core, :, :, :, cols] = result.astype(BF16).reshape(4, 4, PIECE, 512)
 
-            for o in (None,) if q == 0 else (2, 1, 3, 0):
+            for o in (None,) if q == 0 else (2,):
 
                 @pl.loop(0, 4)
                 def _(d):
@@ -366,6 +371,14 @@
                     def _():
                         c1(q, d, dc, o).start()
                         d1(q, d, dc, o).start()
+
+        if q == SPLIT - 1:
+            for o in (1, 3, 0):
+
+                @pl.loop(1, 8)
+                def _(j):
+                    c1(q, j // 2, j % 2, o).start()
+                    d1(q, j // 2, j % 2, o).start()
 
         own(q, 4).start()
         own(q, 5).start()
@@ -397,13 +410,14 @@
         for way in range(2):
             sums(way, 0, axis).start()
     for axis in range(2):
-        several(relay_a.at[0, 0:7, 0:3], ret_recv.at[axis, 1]).wait_recv()
+        several(relay_a.at[0, 0:7, 0:2], ret_recv.at[axis, 1]).wait_recv()
     for way in range(2):
         for axis in range(2):
             store = [sum_a, sum_b][axis]
             store[1 + way] = sum_for([1, 3][way], axis).astype(BF16)
             sums(way, 1, axis).start()
     for axis in range(2):
+        several(relay_a.at[0, 0:7, 0], ret_recv.at[axis, 3]).wait_recv()
         total[:, [low, high][axis]] = sum_for(0, axis)
     for way in range(2):
         for axis in range(2):
@@ -479,8 +493,8 @@
             per_token,
             pltpu.VMEM((ROWS, units), BF16),
             pltpu.VMEM((rows, width), F32),
-            pltpu.VMEM((4, 8, 128), F32),
-            pltpu.VMEM((8, 4, 8, 128), F32),
+            pltpu.VMEM((8, 128), F32),
+            pltpu.VMEM((8, 8, 128), F32),
             pltpu.VMEM((8, 128), F32),
             pltpu.VMEM((8, 128), F32),
             pltpu.VMEM((8, 128), F32),
@@ -495,7 +509,7 @@
             dma((2, 2, 3)),
             dma((4,)),
             dma((2, SPLIT, 2)),
-            dma((2, SPLIT + 1)),
+            dma((2, SPLIT + 2)),
         ],
         compiler_params=pltpu.CompilerParams(
             collective_id=0, has_side_effects=True, vmem_limit_bytes=60 * 2**20

time: 96.8 us -> 95.5 us (0.987)
  Pallas kernels: 93.6 us -> 92.3 us
    pallas_call x1, Pallas kernels: 93.6 us -> 92.3 us  [on_device(): pl.pallas_call(kernel, out_shape=jax.ShapeDtypeStruct((rows, width), BF16...]
where the time goes in v7:
time: 95.5 us; the launch traced here: 95.3 us
  Pallas kernels  92.3 us (97%)
  local copies, waits for them, and re-layouts  2.3 us (2%)
    pallas_call x1, Pallas kernels, on_device(): pl.pallas_call(kernel, out_shape=jax.ShapeDtypeStruct((rows, width), BF16...  92.3 us
    unnamed x1, local copies, waits for them, and re-layouts  2.3 us

profile of v7, /device:TPU:1, one launch (start us, length us, event | category | flops | bytes accessed | tf_op | source)
XLA Modules:
  0.0 95.3 jit_solution(14274311254506308407)
XLA Ops:
  0.7 92.3 %shard_map.73 = bf16[256,2048]{1,0:T(8,128)(2,1)} custom-call(bf16[256,2048]{1,0:T(8,128)(2,1)} %tokens_hbm.1, s32[8,256]{1,0:T(8,128)} %bitcast.2, f32[8,256]{1,0:T(8,128)} %bitcast.3, bf16[1,2048,768]{2,1,0:T(8,128)(2,1)} %w_gate_hbm.1, bf16[1,2048,768]{2,1,0:T(8,128)(2,1)} %w_up_hbm.1, bf16[1,768,2048]{2,1,0:T(8,128)(2,1)} %w_down_hbm.1, ...), custom_call_target="tpu_custom_call" | custom-call | flops 9663676416 | bytes 9437184 | tf_op jit(solution)/shard_map/pallas_call | solution.py:463
  93.0 2.3 %copy.10 = bf16[256,2048]{1,0:T(8,128)(2,1)} copy(bf16[256,2048]{1,0:T(8,128)(2,1)} %shard_map.73) | data formatting | bytes 2097152

commit v8 on v7

--- a/solution.py
+++ b/solution.py
@@ -315,9 +315,11 @@
     for axis in range(2):
         for way in range(2):
             ring(way, 2, axis).wait_recv()
+    start_second(1, 0)
     pack(2)
     start_second(0, 2)
-    start_second(1, None)
+    for o in (3, 1, 2):
+        start_second(1, o)
     for q in range(SPLIT):
         own(q, 2).start()
         own(q, 3).start()

time: 95.5 us -> 95.5 us (level)
  no operation moved by 1% of the time
where the time goes in v8:
time: 95.5 us; the launch traced here: 95.3 us
  Pallas kernels  92.3 us (97%)
  local copies, waits for them, and re-layouts  2.3 us (2%)
    pallas_call x1, Pallas kernels, on_device(): pl.pallas_call(kernel, out_shape=jax.ShapeDtypeStruct((rows, width), BF16...  92.3 us
    unnamed x1, local copies, waits for them, and re-layouts  2.3 us

profile of v8, /device:TPU:1, one launch (start us, length us, event | category | flops | bytes accessed | tf_op | source)
XLA Modules:
  0.0 95.3 jit_solution(12705011347320620446)
XLA Ops:
  0.7 92.3 %shard_map.73 = bf16[256,2048]{1,0:T(8,128)(2,1)} custom-call(bf16[256,2048]{1,0:T(8,128)(2,1)} %tokens_hbm.1, s32[8,256]{1,0:T(8,128)} %bitcast.2, f32[8,256]{1,0:T(8,128)} %bitcast.3, bf16[1,2048,768]{2,1,0:T(8,128)(2,1)} %w_gate_hbm.1, bf16[1,2048,768]{2,1,0:T(8,128)(2,1)} %w_up_hbm.1, bf16[1,768,2048]{2,1,0:T(8,128)(2,1)} %w_down_hbm.1, ...), custom_call_target="tpu_custom_call" | custom-call | flops 9663676416 | bytes 9437184 | tf_op jit(solution)/shard_map/pallas_call | solution.py:465
  93.0 2.3 %copy.10 = bf16[256,2048]{1,0:T(8,128)(2,1)} copy(bf16[256,2048]{1,0:T(8,128)(2,1)} %shard_map.73) | data formatting | bytes 2097152
